TPU v7x, 256 devices: a whole 4x4x8 slice. The times are simulated.
256 devices in a mesh: dp: 16 (over x_lo, z), tensor: 4 (over x_hi, core), latent: 4 (over y).
Axes of the slice: x: 4 (x_hi: 2, x_lo: 2; x = x_hi * 2 + x_lo), y: 4, z: 8, core: 2. Of those that a mesh axis runs over, the one named last changes fastest.
Arguments:
- residual: bfloat16 [2048, 4608], P('dp', ('tensor', 'latent')), may hold values from -6 to 6
- segments: int32 [16, 128], P('dp'), may hold values from 0 to 3, never falling along the last dimension, each value on 1 to 64 neighbouring positions
- row_perm: int32 [2048], P('dp'), may hold values from 0 to 2047, as said below
- pre_gain: float32 [4608], replicated, may hold values from 0.25 to 1.75
- post_gain: float32 [4608], replicated, may hold values from 0.25 to 1.75
- w_query: bfloat16 [4608, 4096], P(None, ('tensor', 'latent')), may hold values from -0.70710678 to 0.70710678
- w_key: bfloat16 [4608, 2048], P(None, ('tensor', 'latent')), may hold values from -0.09375 to 0.09375
- w_value: bfloat16 [4608, 2048], P(None, ('tensor', 'latent')), may hold values from -0.09375 to 0.09375
- w_out: bfloat16 [4096, 4608], P(('tensor', 'latent')), may hold values from -0.09375 to 0.09375
- sae_weight: bfloat16 [4608, 16384], P('dp', ('tensor', 'latent')), may hold values from -0.09375 to 0.09375
- enc_bias: float32 [16384], P(('tensor', 'latent')), may hold values from -3 to 3
- thresholds: float32 [16384], P(('tensor', 'latent')), may hold values from 0.2 to 1.2
- dec_bias: float32 [4608], replicated, may hold values from -3 to 3
Outputs:
- weight_grad: bfloat16 [4608, 16384], P('dp', ('tensor', 'latent'))
- bias_grad: float32 [16384], P(('tensor', 'latent'))
- codes: bfloat16 [2048, 16384], P('dp', ('tensor', 'latent'))
Inputs may be any that keep to these rules, and one draw needn't show every extreme that they name: `segments`: segment numbers never fall along a row. row_perm is a permutation. Within the rows 128 g to 128 (g + 1) - 1, the 8 rows starting at 128 g + s * 8 hold only indices from 128 s to 128 (s + 1) - 1.
All inputs are finite; a program needn't handle non-finite values.
Results may differ from a plain program's by a relative error of at most 0.03.
Values may be sent and summed in bfloat16 or wider, within the bound.
A program may use at most 128 MiB of HBM per device.

v0:
```python
import math

import jax
import jax.numpy as jnp
from jax import lax
from jax.sharding import PartitionSpec as P

D = 4608
HEADS = 32
HEAD = 128


epsilon = 1e-06
softcap = 50.0
ramp_width = 0.05
rotary_base = 10000.0


def split_up(array, dim, size):
    dims = array.shape
    tiles = array.reshape(*dims[:dim], size, dims[dim] // size, *dims[dim + 1 :])
    return jnp.moveaxis(tiles, dim, 0)


def sum_at_owner(array, axis, dim):
    size = lax.axis_size(axis)
    tiles = lax.all_to_all(split_up(array, dim, size), axis, 0, 0, tiled=True)
    return jnp.sum(tiles.astype(jnp.float32), axis=0)


def from_everyone(array, axis):
    copies = jnp.broadcast_to(array, (lax.axis_size(axis), *array.shape))
    return lax.all_to_all(copies, axis, split_axis=0, concat_axis=0, tiled=True)


def taken_together(array, axis):
    return from_everyone(array, axis).sum(axis=0)


def rms_scale(field, gain_vec):
    return field * lax.rsqrt(jnp.mean(field * field, axis=-1, keepdims=True) + epsilon) * gain_vec


def rotate(field, positions):
    half_width = field.shape[-1] // 2
    frequency = rotary_base ** (-2.0 * jnp.arange(half_width, dtype=jnp.float32) / field.shape[-1])
    angles = positions[..., :, None, None] * frequency
    cosine = jnp.cos(angles)
    sine_part = jnp.sin(angles)
    first_half = field[..., :half_width]
    second_half = field[..., half_width:]
    return jnp.concatenate(
        [
            first_half * cosine - second_half * sine_part,
            second_half * cosine + first_half * sine_part,
        ],
        axis=-1,
    )


def doc_masks(segment_ids):
    same_doc = segment_ids[..., :, None] == segment_ids[..., None, :]
    indices = jnp.arange(segment_ids.shape[-1], dtype=jnp.int32)
    earlier = indices[None, :] < indices[:, None]
    positions = jnp.sum((same_doc & earlier).astype(jnp.float32), axis=-1)
    attend_mask = (same_doc & (indices[None, :] <= indices[:, None])).astype(jnp.float32)
    return (positions, attend_mask)


def local(
    residual,
    segments,
    row_perm,
    pre_gain,
    post_gain,
    w_query,
    w_key,
    w_value,
    w_out,
    sae_weight,
    enc_bias,
    thresholds,
    dec_bias,
):
    stream_rows = lax.all_gather(residual, ("tensor", "latent"), axis=1, tiled=True)
    length = stream_rows.shape[0]
    stream = stream_rows.astype(jnp.float32)
    normed = rms_scale(stream, pre_gain).astype(jnp.bfloat16)
    positions, attend_mask = doc_masks(segments[0])
    query_heads = w_query.shape[1] // HEAD
    key_heads = w_key.shape[1] // HEAD
    group_ratio = query_heads // key_heads
    query_projected = jnp.dot(normed, w_query, preferred_element_type=jnp.float32).reshape(
        length, query_heads, HEAD
    )
    query_projected = (
        rotate(query_projected, positions)
        .astype(jnp.bfloat16)
        .reshape(length, key_heads, group_ratio, HEAD)
    )
    key_projected = jnp.dot(normed, w_key, preferred_element_type=jnp.float32).reshape(
        length, key_heads, HEAD
    )
    key_projected = rotate(key_projected, positions).astype(jnp.bfloat16)
    value_projected = (
        jnp.dot(normed, w_value, preferred_element_type=jnp.float32)
        .astype(jnp.bfloat16)
        .reshape(length, key_heads, HEAD)
    )
    logit_matrix = jnp.einsum(
        "zjei,kji->jezk", query_projected, key_projected, preferred_element_type=jnp.float32
    ) * (D / HEADS) ** (-0.5)
    logit_matrix = softcap * jnp.tanh(logit_matrix / softcap)
    weighted = jnp.exp(logit_matrix) * attend_mask
    attention_weights = (weighted / jnp.sum(weighted, axis=-1, keepdims=True)).astype(jnp.bfloat16)
    head_out = jnp.einsum(
        "jzku,ujw->kjzw", attention_weights, value_projected, preferred_element_type=jnp.float32
    )
    head_out = head_out.astype(jnp.bfloat16).reshape(length, query_heads * HEAD)
    partial_value = jnp.dot(head_out, w_out, preferred_element_type=jnp.float32)
    width = residual.shape[1]
    offset = lax.axis_index(("tensor", "latent")) * width
    group_count = lax.axis_size("dp")
    block = length // group_count
    request = (
        row_perm.reshape(group_count, block)
        - (jnp.arange(group_count, dtype=jnp.int32) * length)[:, None]
    )
    wanted = lax.all_to_all(request, "dp", split_axis=0, concat_axis=0, tiled=True)
    attn_part = sum_at_owner(partial_value.astype(jnp.bfloat16), ("tensor", "latent"), 1)
    squares = taken_together(
        jnp.sum(attn_part * attn_part, axis=1, keepdims=True), ("tensor", "latent")
    )
    gain_part = lax.dynamic_slice_in_dim(post_gain, offset, width, 0)
    post_part = attn_part * lax.rsqrt(squares / D + epsilon) * gain_part
    hidden = (residual.astype(jnp.float32) + post_part).astype(jnp.bfloat16)
    sae_part = lax.all_to_all(
        hidden[wanted], "dp", split_axis=0, concat_axis=0, tiled=True
    ).reshape(length, width)
    sae_full = lax.all_gather(sae_part, ("tensor", "latent"), axis=1, tiled=True)
    weights = lax.all_gather(sae_weight, "dp", axis=0, tiled=True)
    pre_acts = jnp.dot(sae_full, weights, preferred_element_type=jnp.float32) + enc_bias
    open_gate = jax.nn.sigmoid((pre_acts - thresholds) / ramp_width)
    latent_acts = (pre_acts * open_gate).astype(jnp.bfloat16)
    contract_last = (((1,), (1,)), ((), ()))
    rebuilt = lax.dot_general(
        latent_acts, weights, contract_last, preferred_element_type=jnp.float32
    )
    rebuilt_part = sum_at_owner(rebuilt.astype(jnp.bfloat16), ("tensor", "latent"), 1)
    bias_part = lax.dynamic_slice_in_dim(dec_bias, offset, width, 0)
    error_part = (rebuilt_part + bias_part - sae_part.astype(jnp.float32)).astype(jnp.bfloat16)
    error_bf = lax.all_gather(error_part, ("tensor", "latent"), axis=1, tiled=True)
    latent_gradient = jnp.dot(error_bf, weights, preferred_element_type=jnp.float32)
    slope = open_gate + pre_acts * open_gate * (1.0 - open_gate) / ramp_width
    grad_pre = (latent_gradient * slope).astype(jnp.bfloat16)
    grad_scale = 1.0 / math.sqrt(length * group_count)
    contract_first = (((0,), (0,)), ((), ()))
    leading_summand = lax.dot_general(
        sae_full, grad_pre, contract_first, preferred_element_type=jnp.float32
    )
    second_term = lax.dot_general(
        error_bf, latent_acts, contract_first, preferred_element_type=jnp.float32
    )
    weight_grad = lax.psum_scatter(
        (grad_scale * (leading_summand + second_term)).astype(jnp.bfloat16),
        "dp",
        scatter_dimension=0,
        tiled=True,
    )
    bias_grad = taken_together(grad_scale * jnp.sum(grad_pre.astype(jnp.float32), axis=0), "dp")
    return (weight_grad, bias_grad, latent_acts)


def solution(mesh):
    return jax.shard_map(
        local,
        mesh=mesh,
        in_specs=(
            P("dp", ("tensor", "latent")),
            P("dp", None),
            P("dp"),
            P(),
            P(),
            P(None, ("tensor", "latent")),
            P(None, ("tensor", "latent")),
            P(None, ("tensor", "latent")),
            P(("tensor", "latent"), None),
            P("dp", ("tensor", "latent")),
            P(("tensor", "latent")),
            P(("tensor", "latent")),
            P(),
        ),
        out_specs=(
            P("dp", ("tensor", "latent")),
            P(("tensor", "latent")),
            P("dp", ("tensor", "latent")),
        ),
        check_vma=False,
    )
```

profile of v0, /device:TPU:1, one launch (start us, length us, event | category | flops | bytes accessed | tf_op | source)
XLA Modules:
  0.0 521.8 jit_solution(14969716449078167956)
XLA Ops:
  7.2 0.7 all-gather.5.cloned.1.call-update
  7.9 0.7 reshape.312
  8.7 0.7 broadcast_subtract_fusion
  9.3 10.1 %all-to-all-start.2 = ((s32[16,1,8]{2,1,0:T(1,128)}), s32[16,1,8]{2,1,0:T(1,128)}, u32[]{:S(2)}, u32[]{:S(2)}) async-start(s32[16,1,8]{2,1,0:T(1,128)} %bitcast.14), calls=%async_computation.2 | async-start | bytes 16384 | tf_op jit(solution)/shard_map/all_to_all | solution.py:129
  19.5 0.8 convert_reduce_fusion.3
  20.3 1.4 fusion.16
  21.7 1.0 multiply_cosine_fusion
  22.7 42.7 %all-gather.5.cloned.1.call-done = bf16[128,4608]{0,1:T(8,128)(2,1)} async-done(((bf16[128,288]{0,1:T(8,128)(2,1)}), bf16[128,4608]{0,1:T(8,128)(2,1)}) %all-gather.5.cloned.1.call-update) | async-done | bytes 1179664 | tf_op jit(solution)/shard_map/all_gather | solution.py:85
  65.4 2.0 fusion
  67.4 2.8 convolution_bitcast_fusion
  70.2 0.8 fusion.28
  71.1 1.9 fusion.30
  73.0 1.6 reshape.308
  74.6 1.2 fusion.35
  75.8 0.9 subtract_convert_fusion.1
  76.7 2.4 fusion.36
  79.0 3.4 convolution_convert_fusion.2
  82.4 1.3 convolution_convert_fusion.1
  83.8 1.4 copy.93
  85.2 3.9 all-to-all-start
  89.1 1.4 dynamic_slice.6
  90.5 0.8 copy.95
  92.0 15.1 %all-to-all-done = bf16[16,128,288]{1,2,0:T(8,128)(2,1)S(1)} async-done(((bf16[16,128,288]{1,2,0:T(8,128)(2,1)}), bf16[16,128,288]{1,2,0:T(8,128)(2,1)S(1)}, u32[]{:S(2)}, u32[]{:S(2)}) %all-to-all-start) | async-done | bytes 1179680 | tf_op jit(solution)/shard_map/all_to_all | solution.py:27
  107.3 0.7 copy-done.8
  108.6 4.8 all-to-all-start.1
  114.0 6.2 %all-to-all-done.1 = f32[16,128,1]{1,2,0:T(1,128)S(1)} async-done(((f32[16,128,1]{1,2,0:T(1,128)}), f32[16,128,1]{1,2,0:T(1,128)S(1)}, u32[]{:S(2)}, u32[]{:S(2)}) %all-to-all-start.1) | async-done | bytes 8224 | tf_op jit(solution)/shard_map/all_to_all | solution.py:33
  120.3 1.1 add_convert_fusion
  121.5 0.9 gather_fusion
  122.4 15.0 %all_to_all.35 = bf16[16,8,288]{2,1,0:T(8,128)(2,1)S(1)} all-to-all(bf16[16,8,288]{2,1,0:T(8,128)(2,1)S(1)} %bitcast.60), channel_id=1, replica_groups=mesh['dp'=16,'tensor'=4,'latent'=4] {'dp'}, dimensions={0} | all-to-all | bytes 147456 | tf_op jit(solution)/shard_map/all_to_all | solution.py:137
  137.3 0.7 copy.98
  138.2 0.7 all-gather.9.cloned.1.call-update
  138.8 44.9 %all-gather.7.cloned.1.call-done = bf16[128,4608]{0,1:T(8,128)(2,1)} async-done(((bf16[128,288]{0,1:T(8,128)(2,1)}), bf16[128,4608]{0,1:T(8,128)(2,1)}) %all-gather.7.cloned.1.call-update) | async-done | bytes 1179664 | tf_op jit(solution)/shard_map/all_gather | solution.py:140
  183.7 111.7 %all-gather.9.cloned.1.call-done = bf16[4608,1024]{1,0:T(8,128)(2,1)} async-done(((bf16[288,1024]{1,0:T(8,128)(2,1)}), bf16[4608,1024]{1,0:T(8,128)(2,1)}) %all-gather.9.cloned.1.call-update) | async-done | bytes 9437200 | tf_op jit(solution)/shard_map/all_gather | solution.py:141
  295.5 6.5 %fusion.11 = (bf16[128,1024]{1,0:T(8,128)(2,1)S(1)}, f32[128,1024]{1,0:T(8,128)}) fusion(f32[1024]{0:T(1024)S(1)} %copy-done.10, f32[1024]{0:T(1024)S(1)} %copy-done.11, bf16[128,4608]{0,1:T(8,128)(2,1)} %all-gather.7.cloned.1.call-done, bf16[4608,1024]{1,0:T(8,128)(2,1)} %all-gather.9.cloned.1.call-done), kind=kOutput, calls=%fused_computation.27 | convolution fusion | flops 1209008128 | bytes 11411456 | tf_op jit(solution)/shard_map/dot_general | solution.py:142
  301.9 0.7 copy-done.5
  302.6 3.2 convolution_convert_fusion
  305.8 1.4 copy.99
  307.2 7.1 %all-to-all-start.4 = ((bf16[16,128,288]{1,2,0:T(8,128)(2,1)}), bf16[16,128,288]{1,2,0:T(8,128)(2,1)S(1)}, u32[]{:S(2)}, u32[]{:S(2)}) async-start(bf16[16,128,288]{1,2,0:T(8,128)(2,1)} %bitcast.59), calls=%async_computation.4 | async-start | bytes 2359296 | tf_op jit(solution)/shard_map/all_to_all | solution.py:27
  314.4 0.8 dynamic_slice.7
  315.2 17.2 %all-to-all-done.4 = bf16[16,128,288]{1,2,0:T(8,128)(2,1)S(1)} async-done(((bf16[16,128,288]{1,2,0:T(8,128)(2,1)}), bf16[16,128,288]{1,2,0:T(8,128)(2,1)S(1)}, u32[]{:S(2)}, u32[]{:S(2)}) %all-to-all-start.4) | async-done | bytes 1179680 | tf_op jit(solution)/shard_map/all_to_all | solution.py:27
  332.5 1.6 subtract_convert_fusion
  334.3 46.0 %all-gather.11.cloned.1.call-done = bf16[128,4608]{0,1:T(8,128)(2,1)} async-done(((bf16[128,288]{0,1:T(8,128)(2,1)}), bf16[128,4608]{0,1:T(8,128)(2,1)}) %all-gather.11.cloned.1.call-update) | async-done | bytes 1179664 | tf_op jit(solution)/shard_map/all_gather | solution.py:152
  380.4 5.7 %convert_reduce_fusion.2 = (f32[1024]{0:T(1024)S(1)}, bf16[128,1024]{1,0:T(8,128)(2,1)S(1)}) fusion(f32[128,1024]{1,0:T(8,128)} %get-tuple-element.14, f32[1024]{0:T(1024)S(1)} %copy-done.10, bf16[128,4608]{0,1:T(8,128)(2,1)} %all-gather.11.cloned.1.call-done, bf16[4608,1024]{1,0:T(8,128)(2,1)} %all-gather.9.cloned.1.call-done), kind=kOutput, calls=%fused_computation.24 | convolution fusion | flops 1209793536 | bytes 11411456 | tf_op jit(solution)/shard_map/dot_general | solution.py:153
  386.1 7.9 %fusion.37 = f32[4608,1024]{1,0:T(8,128)} fusion(bf16[128,4608]{0,1:T(8,128)(2,1)S(1)} %copy-done.2, bf16[128,1024]{1,0:T(8,128)(2,1)S(1)} %get-tuple-element.16), kind=kOutput, calls=%fused_computation.73 | convolution fusion | flops 1207959552 | bytes 20316160 | tf_op jit(solution)/shard_map/dot_general | solution.py:158
  394.0 10.7 %multiply_convert_fusion = bf16[4608,1024]{1,0:T(8,128)(2,1)} fusion(f32[4608,1024]{1,0:T(8,128)} %fusion.37, bf16[128,4608]{0,1:T(8,128)(2,1)S(1)} %copy-done.3, bf16[128,1024]{1,0:T(8,128)(2,1)S(1)} %copy-done.6), kind=kOutput, calls=%fused_computation.1 | convolution fusion | flops 1222115328 | bytes 29753344 | tf_op jit(solution)/shard_map/dot_general | solution.py:161
  404.7 14.0 %all_to_all.36 = f32[16,1,1024]{2,1,0:T(1,128)S(1)} all-to-all(f32[16,1,1024]{2,1,0:T(1,128)S(1)} %broadcast_in_dim.5), channel_id=1, replica_groups=mesh['dp'=16,'tensor'=4,'latent'=4] {'dp'}, dimensions={0} | all-to-all | bytes 131072 | tf_op jit(solution)/shard_map/all_to_all | solution.py:33
  418.7 0.6 reduce_sum.89
  419.4 95.9 %reduce-scatter.2.cloned.1.call-done = bf16[288,1024]{1,0:T(8,128)(2,1)} async-done(((bf16[4608,1024]{1,0:T(8,128)(2,1)}), bf16[288,1024]{1,0:T(8,128)(2,1)}) %reduce-scatter.2.cloned.1.call-update) | async-done | bytes 589840 | tf_op jit(solution)/shard_map/reduce_scatter | solution.py:164
  (57 shorter events, 3.0 us)
Async XLA Ops:
  7.2 75.3 %copy-start = (bf16[256,4608]{1,0:T(8,128)(2,1)S(1)}, bf16[256,4608]{1,0:T(8,128)(2,1)}, u32[]{:S(2)}) copy-start(bf16[256,4608]{1,0:T(8,128)(2,1)} %param.21) | copy-start | bytes 7077892
  7.2 58.2 %all-gather.5.cloned.1.call-start = ((), (), s32[]{:S(2)}) async-start(), calls=%async_computation.7 | async-start | bytes 1253376 | tf_op jit(solution)/shard_map/all_gather | solution.py:85
  9.3 75.9 %all-to-all-start.2 = ((s32[16,1,8]{2,1,0:T(1,128)}), s32[16,1,8]{2,1,0:T(1,128)}, u32[]{:S(2)}, u32[]{:S(2)}) async-start(s32[16,1,8]{2,1,0:T(1,128)} %bitcast.14), calls=%async_computation.2 | async-start | bytes 16384 | tf_op jit(solution)/shard_map/all_to_all | solution.py:129
  19.5 2.3 copy-start.12
  20.3 1.4 copy-start.14
  65.3 4.9 copy-start.13
  65.3 4.9 copy-start.15
  65.3 5.7 %copy-start.4 = (bf16[128,4608]{0,1:T(8,128)(2,1)S(1)}, bf16[128,4608]{0,1:T(8,128)(2,1)}, u32[]{:S(2)}) copy-start(bf16[128,4608]{0,1:T(8,128)(2,1)} %all-gather.5.cloned.1.call-done) | copy-start | bytes 3538948
  65.4 5.7 %copy-start.7 = (bf16[4608,256]{1,0:T(8,128)(2,1)S(1)}, bf16[4608,256]{1,0:T(8,128)(2,1)}, u32[]{:S(2)}) copy-start(bf16[4608,256]{1,0:T(8,128)(2,1)} %param.18) | copy-start | bytes 7077892
  65.4 5.7 %copy-start.9 = (f32[4608]{0:T(1024)S(1)}, f32[4608]{0:T(1024)}, u32[]{:S(2)}) copy-start(f32[4608]{0:T(1024)} %param.16) | copy-start | bytes 55300
  67.4 3.6 copy-start.16
  85.2 21.9 %all-to-all-start = ((bf16[16,128,288]{1,2,0:T(8,128)(2,1)}), bf16[16,128,288]{1,2,0:T(8,128)(2,1)S(1)}, u32[]{:S(2)}, u32[]{:S(2)}) async-start(bf16[16,128,288]{1,2,0:T(8,128)(2,1)} %bitcast.58), calls=%async_computation | async-start | bytes 2359296 | tf_op jit(solution)/shard_map/all_to_all | solution.py:27
  89.1 206.3 %copy-start.10 = (f32[1024]{0:T(1024)S(1)}, f32[1024]{0:T(1024)}, u32[]{:S(2)}) copy-start(f32[1024]{0:T(1024)} %param.24) | copy-start | bytes 12292
  91.3 204.1 %copy-start.11 = (f32[1024]{0:T(1024)S(1)}, f32[1024]{0:T(1024)}, u32[]{:S(2)}) copy-start(f32[1024]{0:T(1024)} %param.23) | copy-start | bytes 12292
  107.3 0.7 copy-start.8
  108.6 11.7 %all-to-all-start.1 = ((f32[16,128,1]{1,2,0:T(1,128)}), f32[16,128,1]{1,2,0:T(1,128)S(1)}, u32[]{:S(2)}, u32[]{:S(2)}) async-start(f32[16,128,1]{1,2,0:T(1,128)} %broadcast_in_dim.4), calls=%async_computation.1 | async-start | bytes 16384 | tf_op jit(solution)/shard_map/all_to_all | solution.py:33
  113.4 70.4 %all-gather.7.cloned.1.call-start = ((), (), s32[]{:S(2)}) async-start(), calls=%async_computation.8 | async-start | bytes 1253376 | tf_op jit(solution)/shard_map/all_gather | solution.py:140
  138.1 157.4 %all-gather.9.cloned.1.call-start = ((), (), s32[]{:S(2)}) async-start(), calls=%async_computation.9 | async-start | bytes 10027008 | tf_op jit(solution)/shard_map/all_gather | solution.py:141
  295.5 7.2 %copy-start.1 = (bf16[4608,1024]{1,0:T(8,128)(2,1)S(1)}, bf16[4608,1024]{1,0:T(8,128)(2,1)}, u32[]{:S(2)}) copy-start(bf16[4608,1024]{1,0:T(8,128)(2,1)} %all-gather.9.cloned.1.call-done) | copy-start | bytes 28311556
  301.9 0.7 copy-start.5
  307.2 25.1 %all-to-all-start.4 = ((bf16[16,128,288]{1,2,0:T(8,128)(2,1)}), bf16[16,128,288]{1,2,0:T(8,128)(2,1)S(1)}, u32[]{:S(2)}, u32[]{:S(2)}) async-start(bf16[16,128,288]{1,2,0:T(8,128)(2,1)} %bitcast.59), calls=%async_computation.4 | async-start | bytes 2359296 | tf_op jit(solution)/shard_map/all_to_all | solution.py:27
  314.3 66.0 %all-gather.11.cloned.1.call-start = ((), (), s32[]{:S(2)}) async-start(), calls=%async_computation.10 | async-start | bytes 1253376 | tf_op jit(solution)/shard_map/all_gather | solution.py:152
  334.1 181.1 %reduce-scatter.2.cloned.1.call-start = ((), (), s32[]{:S(2)}) async-start(), calls=%async_computation.11 | async-start | bytes 10027008 | tf_op jit(solution)/shard_map/reduce_scatter | solution.py:164
  380.4 5.7 %copy-start.2 = (bf16[128,4608]{0,1:T(8,128)(2,1)S(1)}, bf16[128,4608]{0,1:T(8,128)(2,1)}, u32[]{:S(2)}) copy-start(bf16[128,4608]{0,1:T(8,128)(2,1)} %all-gather.7.cloned.1.call-done) | copy-start | bytes 3538948
  386.1 7.9 %copy-start.3 = (bf16[128,4608]{0,1:T(8,128)(2,1)S(1)}, bf16[128,4608]{0,1:T(8,128)(2,1)}, u32[]{:S(2)}) copy-start(bf16[128,4608]{0,1:T(8,128)(2,1)} %all-gather.11.cloned.1.call-done) | copy-start | bytes 3538948
  386.1 7.9 %copy-start.6 = (bf16[128,1024]{1,0:T(8,128)(2,1)S(1)}, bf16[128,1024]{1,0:T(8,128)(2,1)}, u32[]{:S(2)}) copy-start(bf16[128,1024]{1,0:T(8,128)(2,1)} %copy-done.5) | copy-start | bytes 786436
Sparse Core Ops, SparseCore 0:
  10.8 54.5 all-gather.4
  138.2 45.4 all-gather.6
  185.5 109.8 all-gather.8
  334.2 46.0 all-gather.10
  404.8 110.4 reduce-scatter.1
where the time goes:
time: 523 us; the launch traced here: 522 us
  waiting for transfers between devices  381 us (73%)
  matrix products  45.7 us (9%)
  blocking collectives  29 us (6%)
  starting transfers between devices  26.3 us (5%)
  between operations  14 us (3%)
  local copies, waits for them, and re-layouts  13.7 us (3%)
  other arithmetic  12.1 us (2%)
    all_gather x1, waiting for transfers between devices, local(): weights = lax.all_gather(sae_weight, 'dp', axis=0, tiled=True)  112 us
    reduce_scatter x1, waiting for transfers between devices, local(): lax.psum_scatter((grad_scale * (leading_summand + second_term)).astype(jn...  95.9 us
    all_gather x1, waiting for transfers between devices, local(): lax.all_gather(error_part, ('tensor', 'latent'), axis=1, tiled=True)  46 us
    all_gather x1, waiting for transfers between devices, local(): lax.all_gather(sae_part, ('tensor', 'latent'), axis=1, tiled=True)  44.9 us
    all_gather x1, waiting for transfers between devices, local(): lax.all_gather(residual, ('tensor', 'latent'), axis=1, tiled=True)  42.7 us
    all_to_all x2, waiting for transfers between devices, sum_at_owner(): tiles = lax.all_to_all(split_up(array, dim, size), axis, 0, 0, tiled=True)  32.3 us
    all_to_all x1, blocking collectives, local(): lax.all_to_all(hidden[wanted], 'dp', split_axis=0, concat_axis=0, tiled=T...  15 us
    all_to_all x1, blocking collectives, from_everyone(): return lax.all_to_all(copies, axis, split_axis=0, concat_axis=0, tiled=True)  14 us
  transfers between devices with their start and end apart: 9, of which 8 were waited for; matrix products, arithmetic and copies ran while one was open for 6% of the time, Pallas kernels for 0%

commit v1 on v0

v1 whole, which is shorter than its diff:
```python
import math

import jax
import jax.numpy as jnp
from jax import lax
from jax.experimental import pallas as pl
from jax.experimental.pallas import tpu as pltpu
from jax.sharding import PartitionSpec as P

D = 4608
HEADS = 32
HEAD = 128
LANES = 1024
TOK = 128
GROUPS = 16
TOKENS = TOK * GROUPS
BLOCK = 8
WIDTH = D // 16
SEMS = 300

epsilon = 1e-06
softcap = 50.0
ramp_width = 0.05
rotary_base = 10000.0

MESH = pl.DeviceIdType.MESH
F32 = jnp.float32
BF16 = jnp.bfloat16
ROW_BY_ROW = (((1,), (1,)), ((), ()))


def dot(a, b):
    return jnp.dot(a, b, preferred_element_type=F32)


def dot_t(a, b):
    return lax.dot_general(a, b, ROW_BY_ROW, preferred_element_type=F32)


class Place:
    def __init__(self):
        self.dp = lax.axis_index("dp")
        self.ten = lax.axis_index("tensor")
        self.lat = lax.axis_index("latent")
        self.xl, self.z = self.dp // 8, self.dp % 8
        self.xh, self.core = self.ten // 2, self.ten % 2
        self.t = self.ten * 4 + self.lat

    def at(self, dp=None, ten=None, lat=None):
        return {
            "dp": self.dp if dp is None else dp,
            "tensor": self.ten if ten is None else ten,
            "latent": self.lat if lat is None else lat,
        }

    def chip(self, k, sign=1):
        return (self.xh + k // 4) % 2, (self.lat + sign * (k % 4) + 4) % 4

    def piece(self, k, core, sign=1):
        xh, y = self.chip(k, sign)
        return (xh * 2 + core) * 4 + y

    def peer(self, k, core=None):
        xh, y = self.chip(k)
        return self.at(ten=xh * 2 + (self.core if core is None else core), lat=y)

    def sibling(self):
        return self.at(ten=self.xh * 2 + 1 - self.core)


class Net:
    def __init__(self, send, recv):
        self.send, self.recv, self.used, self.open = send, recv, 0, []

    def copy(self, src, dst, device):
        i = self.used
        self.used += 1
        assert i < SEMS
        c = pltpu.make_async_remote_copy(
            src_ref=src,
            dst_ref=dst,
            send_sem=self.send.at[i],
            recv_sem=self.recv.at[i],
            device_id=device,
            device_id_type=MESH,
        )
        self.open.append(c)
        return c

    def close(self):
        for c in self.open:
            c.wait_send()
        self.open = []


FAR_FIRST = (6, 5, 7, 4, 2, 1, 3)
NEAR_FIRST = (1, 3, 2, 4, 5, 7, 6)


class Gather:
    def __init__(self, net, me, buf):
        self.net, self.me, self.buf = net, me, buf

    def rows(self, index):
        return self.buf.at[pl.ds(pl.multiple_of(index * WIDTH, 32), WIDTH)]

    def start(self):
        me, own = self.me, self.rows(self.me.t)
        self.far = {}
        for k in FAR_FIRST:
            self.far[k] = self.net.copy(own, own, me.peer(k))
            self.far[k].start()
        self.near = {0: self.net.copy(own, own, me.sibling())}
        self.near[0].start()

    def finish(self):
        me = self.me
        for k in NEAR_FIRST:
            self.far[k].wait_recv()
            got = self.rows(me.piece(k, me.core, -1))
            self.near[k] = self.net.copy(got, got, me.sibling())
            self.near[k].start()
        for k in (0, *NEAR_FIRST):
            self.near[k].wait_recv()


def reduce_to_owner(net, me, part, mate, out, got):
    def rows(ref, index):
        return ref.at[pl.ds(pl.multiple_of(index * WIDTH, 32), WIDTH)]

    order = (*FAR_FIRST, 0)
    pair = {}
    for k in order:
        pair[k] = net.copy(rows(part, me.piece(k, 1 - me.core)), mate.at[k], me.sibling())
        pair[k].start()
    away = {}
    for k in order:
        pair[k].wait_recv()
        both = rows(part, me.piece(k, me.core))[...].astype(F32) + mate[k].astype(F32)
        if k == 0:
            total = both
        else:
            out[k] = both.astype(BF16)
            away[k] = net.copy(out.at[k], got.at[k], me.peer(k))
            away[k].start()
    for k in NEAR_FIRST:
        away[k].wait_recv()
        total = total + got[k].astype(F32)
    return total


class Ring:
    def __init__(self, net, me, buf, size, cut, half_a, half_b):
        self.net, self.me, self.buf, self.size = net, me, buf, size
        self.parts = {
            "a": (me.xl, 0, cut, half_a),
            "b": (me.xl, cut, size - cut, half_b),
            "c": (1 - me.xl, cut, size - cut, half_b),
        }
        self.moves, self.cross = {}, {}

    def rows(self, block, lo, count):
        return self.buf.at[pl.ds(pl.multiple_of(block * self.size + lo, 16), count)]

    def range(self, part, sign, step):
        _, lo, count, half = self.parts[part]
        if step < 4:
            return lo, count
        return (lo, half) if sign > 0 else (lo + half, count - half)

    def move(self, part, sign, step):
        me = self.me
        lo, count = self.range(part, sign, step)
        block = self.parts[part][0] * 8 + (me.z - sign * (step - 1) + 8) % 8
        ref = self.rows(block, lo, count)
        c = self.net.copy(ref, ref, me.at(dp=me.xl * 8 + (me.z + sign + 8) % 8))
        c.start()
        self.moves[part, sign, step] = c

    def over(self, name, block, lo, count):
        me = self.me
        ref = self.rows(block, lo, count)
        c = self.net.copy(ref, ref, me.at(dp=(1 - me.xl) * 8 + me.z))
        c.start()
        self.cross[name] = c

    def start(self):
        _, lo, count, _ = self.parts["b"]
        self.over("b", self.me.dp, lo, count)
        for part in "ab":
            for sign in (1, -1):
                self.move(part, sign, 1)
        _, lo, count, _ = self.parts["a"]
        self.over("a", self.me.dp, lo, count)

    def tick(self, step):
        if step == 0:
            self.cross["b"].wait_recv()
            for sign in (1, -1):
                self.move("c", sign, 1)
            return
        for part in "abc":
            for sign in (1, -1):
                self.moves[part, sign, step].wait_recv()
                if step < 4:
                    self.move(part, sign, step + 1)
                if part == "a":
                    lo, count = self.range(part, sign, step)
                    block = self.me.xl * 8 + (self.me.z - sign * step + 8) % 8
                    self.over((sign, step), block, lo, count)

    def crossed(self):
        for name, c in self.cross.items():
            if name != "b":
                c.wait_recv()


def transpose_into(src, dst):
    @pl.loop(0, D // TOK)
    def _(i):
        at = pl.multiple_of(i * TOK, TOK)
        dst[:, pl.ds(at, TOK)] = src[pl.ds(at, TOK), :].T


def body(
    res,
    seg,
    perm,
    pre_gain,
    gain_col,
    wq_hbm,
    wk_hbm,
    wv_hbm,
    wo_hbm,
    w_hbm,
    enc_bias,
    thr,
    bias_col,
    wg_out,
    bg_out,
    codes_out,
    wq,
    wk,
    wv,
    wo,
    w,
    feat,
    rows,
    part,
    mate,
    out,
    got,
    part2,
    mate2,
    out2,
    got2,
    asked,
    squares,
    sent,
    taken,
    sae_f,
    err_f,
    sae_mine,
    err_mine,
    turned_s,
    turned_e,
    sae_t,
    err_t,
    pre,
    gate,
    codes,
    grads,
    wg,
    final,
    bg,
    local_sem,
    send_sem,
    recv_sem,
):
    me = Place()
    net = Net(send_sem, recv_sem)

    loads = []
    for i, (src, dst) in enumerate(
        [
            (w_hbm, w.at[pl.ds(pl.multiple_of(me.dp * WIDTH, 32), WIDTH)]),
            (wq_hbm, wq),
            (wk_hbm, wk),
            (wv_hbm, wv),
            (wo_hbm, wo),
        ]
    ):
        loads.append(pltpu.make_async_copy(src, dst, local_sem.at[i]))
        loads[-1].start()

    turn_to = me.at(dp=me.t, ten=((me.dp + 1) % 16) // 4, lat=((me.dp + 1) % 16) % 4)
    before = (me.t + 15) % 16
    turn_from = me.at(dp=before, ten=me.dp // 4, lat=me.dp % 4)

    barrier = pltpu.get_barrier_semaphore()
    greeted = [turn_from]
    for k in range(8):
        for core in range(2):
            if k == 0:
                continue
            greeted.append(me.peer(k, core))
    greeted.append(me.sibling())

    def dp_peer(j):
        return ((me.xl + j // 8) % 2) * 8 + (me.z + j % 8) % 8

    for j in range(1, 16):
        greeted.append(me.at(dp=dp_peer(j)))
    for device in greeted:
        pl.semaphore_signal(barrier, inc=1, device_id=device, device_id_type=MESH)
    pl.semaphore_wait(barrier, len(greeted))

    feat[pl.ds(pl.multiple_of(me.t * WIDTH, 32), WIDTH), :] = res[...]
    gather = Gather(net, me, feat)
    gather.start()

    def asked_rows(index):
        return asked.at[pl.ds(pl.multiple_of(index * 8, 8), 8)]

    asked_rows(me.dp)[...] = jnp.broadcast_to(perm[...], (8, TOK))
    asks = []
    for j in range(1, 16):
        asks.append(net.copy(asked_rows(me.dp), asked_rows(me.dp), me.at(dp=dp_peer(j))))
        asks[-1].start()

    loads[0].wait()
    ring = Ring(net, me, w, WIDTH, 176, 96, 48)
    ring.start()

    lane = lax.broadcasted_iota(jnp.int32, (TOK, TOK), 1)
    row = lax.broadcasted_iota(jnp.int32, (TOK, TOK), 0)
    seg_k = jnp.broadcast_to(seg[...].astype(F32), (TOK, TOK))
    same = seg_k == seg_k.T
    position = jnp.sum(jnp.where(same & (lane < row), 1.0, 0.0), axis=1, keepdims=True)
    allowed = same & (lane <= row)
    step = (lane % 64).astype(F32)
    angle = position * jnp.exp(step * (-2.0 / HEAD * math.log(rotary_base)))
    cosine = jnp.cos(angle)
    sine = jnp.sin(angle)
    sine = jnp.where(lane < 64, -sine, sine)

    for c in asks:
        c.wait_recv()
    place = 8 * me.dp + row % 8
    mine = jnp.where(lane == place, asked[...], 0).astype(F32)
    number = jnp.sum(mine, axis=1, keepdims=True) - (me.dp * TOK).astype(F32)
    pick = jnp.where(number == lane.astype(F32), 1.0, 0.0).astype(BF16)

    gather.finish()
    ring.tick(0)
    transpose_into(feat, rows)

    def add_squares(i, acc):
        x = rows[:, pl.ds(pl.multiple_of(i * TOK, TOK), TOK)].astype(F32)
        return acc + x * x

    acc = lax.fori_loop(0, D // TOK, add_squares, jnp.zeros((TOK, TOK), F32), unroll=4)
    scale = lax.rsqrt(jnp.sum(acc, axis=1, keepdims=True) * (1.0 / D) + epsilon)

    @pl.loop(0, D // TOK, unroll=4)
    def _(i):
        at = pl.ds(pl.multiple_of(i * TOK, TOK), TOK)
        rows[:, at] = (rows[:, at].astype(F32) * scale * pre_gain[:, at]).astype(BF16)

    for c in loads[1:]:
        c.wait()
    normed = rows[...]
    query = dot(normed, wq[...])
    key = dot(normed, wk[...])
    value = dot(normed, wv[...]).astype(BF16)

    def rotate(v):
        return (v * cosine + pltpu.roll(v, 64, 1) * sine).astype(BF16)

    key = rotate(key)
    heads = []
    for h in range(2):
        q = rotate(query[:, h * HEAD : (h + 1) * HEAD])
        scores = dot_t(q, key) * (D / HEADS) ** (-0.5)
        scores = softcap * jnp.tanh(scores / softcap)
        weighted = jnp.where(allowed, jnp.exp(scores), 0.0)
        probs = (weighted / jnp.sum(weighted, axis=1, keepdims=True)).astype(BF16)
        heads.append(dot(probs, value).astype(BF16))
    heads = jnp.concatenate(heads, axis=1)

    ring.tick(1)

    @pl.loop(0, D // 256)
    def _(i):
        at = pl.multiple_of(i * 256, 256)
        part[pl.ds(at, 256), :] = dot(heads, wo[:, pl.ds(at, 256)]).astype(BF16).T

    attn = reduce_to_owner(net, me, part, mate, out, got)

    def square_rows(index):
        return squares.at[pl.ds(pl.multiple_of(index * 8, 8), 8)]

    own = jnp.sum(attn * attn, axis=0, keepdims=True)
    square_rows(me.t)[...] = jnp.broadcast_to(own, (8, TOK))
    sums = []
    for k in range(8):
        for core in range(2):
            if k == 0 and core == 0:
                continue
            device = me.peer(k, (me.core + core) % 2)
            sums.append(net.copy(square_rows(me.t), square_rows(me.t), device))
            sums[-1].start()
    ring.tick(2)
    for c in sums:
        c.wait_recv()
    total = jnp.sum(squares[...], axis=0, keepdims=True) * (0.125 / D)
    hidden = res[...].astype(F32) + attn * lax.rsqrt(total + epsilon) * gain_col[...]
    hidden = hidden.astype(BF16)

    low = dot_t(pick, hidden[:256])
    high = dot_t(pick, hidden[32:])
    for g in range(GROUPS):
        block = jnp.concatenate([low[8 * g : 8 * g + 8], high[8 * g : 8 * g + 8]], axis=0)
        sent[g] = block.astype(BF16)
    taken[me.dp] = sent[me.dp]
    moves = []
    for j in range(1, 16):
        to = dp_peer(j)
        moves.append(net.copy(sent.at[to], taken.at[me.dp], me.at(dp=to)))
        moves[-1].start()
    for c in moves:
        c.wait_recv()
    low, high = [], []
    for g in range(GROUPS):
        block = taken[g].astype(F32)
        low.append(block[:8])
        high.append(block[8:, 128:])
    low = jnp.concatenate(low, axis=0)
    high = jnp.concatenate(high, axis=0)
    sae_part = jnp.concatenate([low.T, high.T[96:]], axis=0)
    sae_mine[...] = sae_part.astype(BF16)

    def feature_rows(ref, index):
        return ref.at[pl.ds(pl.multiple_of(index * WIDTH, 32), WIDTH)]

    feature_rows(sae_f, me.t)[...] = sae_mine[...]
    gather = Gather(net, me, sae_f)
    gather.start()
    turn_s = net.copy(sae_mine, turned_s, turn_to)
    turn_s.start()
    gather.finish()
    ring.tick(3)
    transpose_into(sae_f, rows)
    turn_s.wait_recv()
    feature_rows(sae_t, me.t)[...] = turned_s[...]
    gather_st = Gather(net, me, sae_t)
    gather_st.start()
    ring.tick(4)
    ring.crossed()

    ring_c = Ring(net, me, codes, TOK, 80, 48, 32)
    my_rows = pl.ds(pl.multiple_of(me.dp * TOK, TOK), TOK)

    @pl.loop(0, LANES // 256)
    def _(i):
        at = pl.ds(pl.multiple_of(i * 256, 256), 256)
        acts = dot(rows[...], w[:, at]) + enc_bias[:, at]
        opened = jax.nn.sigmoid((acts - thr[:, at]) / ramp_width)
        pre[:, at] = acts
        gate[:, at] = opened
        codes[my_rows, at] = (acts * opened).astype(BF16)

    ring_c.start()
    save_codes = pltpu.make_async_copy(codes.at[my_rows], codes_out, local_sem.at[5])
    save_codes.start()
    mine = codes[my_rows, :]

    @pl.loop(0, 16)
    def _(i):
        at = pl.ds(pl.multiple_of(i * WIDTH, 32), WIDTH)
        part2[at, :] = dot_t(w[at, :], mine).astype(BF16)

    ring_c.tick(0)
    gather_st.finish()
    rebuilt = reduce_to_owner(net, me, part2, mate2, out2, got2)
    error = (rebuilt + bias_col[...] - sae_mine[...].astype(F32)).astype(BF16)
    err_mine[...] = error
    feature_rows(err_f, me.t)[...] = error
    gather = Gather(net, me, err_f)
    gather.start()
    turn_e = net.copy(err_mine, turned_e, turn_to)
    turn_e.start()
    ring_c.tick(1)
    gather.finish()
    turn_e.wait_recv()
    feature_rows(err_t, me.t)[...] = turned_e[...]
    gather_et = Gather(net, me, err_t)
    gather_et.start()
    transpose_into(err_f, rows)

    @pl.loop(0, LANES // 256)
    def _(i):
        at = pl.ds(pl.multiple_of(i * 256, 256), 256)
        opened = gate[:, at]
        slope = opened + pre[:, at] * opened * (1.0 - opened) / ramp_width
        grads[my_rows, at] = (dot(rows[...], w[:, at]) * slope).astype(BF16)

    ring_g = Ring(net, me, grads, TOK, 80, 48, 32)
    ring_g.start()
    ring_c.tick(2)
    ring_g.tick(0)
    gather_et.finish()
    ring_c.tick(3)
    ring_c.tick(4)
    ring_c.crossed()
    wg[...] = jnp.zeros_like(wg)

    def accumulate(features, table):
        @pl.loop(0, GROUPS // 4)
        def _(i):
            left = jnp.concatenate(
                [features[pl.ds(pl.multiple_of(((4 * i + j + 1) % 16) * WIDTH, 32), WIDTH), :] for j in range(4)],
                axis=1,
            )

            @pl.loop(0, LANES // 256)
            def _(n):
                at = pl.ds(pl.multiple_of(n * 256, 256), 256)
                wg[:, at] += dot(left, table[pl.ds(pl.multiple_of(i * 4 * TOK, TOK), 4 * TOK), at])

    accumulate(err_t, codes)
    for s in range(1, 5):
        ring_g.tick(s)
    ring_g.crossed()
    accumulate(sae_t, grads)

    grad_scale = 1.0 / math.sqrt(TOKENS)

    def add_rows(i, acc):
        block = grads[pl.ds(pl.multiple_of(i * TOK, TOK), TOK), :].astype(F32)
        return acc + jnp.sum(block, axis=0, keepdims=True)

    bg[...] = grad_scale * lax.fori_loop(0, GROUPS, add_rows, jnp.zeros((1, LANES), F32))
    final[...] = (wg[...] * grad_scale).astype(BF16)
    save_wg = pltpu.make_async_copy(final, wg_out, local_sem.at[6])
    save_wg.start()
    save_bg = pltpu.make_async_copy(bg, bg_out, local_sem.at[7])
    save_bg.start()
    net.close()
    save_codes.wait()
    save_wg.wait()
    save_bg.wait()


def local(
    residual,
    segments,
    row_perm,
    pre_gain,
    post_gain,
    w_query,
    w_key,
    w_value,
    w_out,
    sae_weight,
    enc_bias,
    thresholds,
    dec_bias,
):
    t = lax.axis_index(("tensor", "latent"))

    def column(v):
        mine = lax.dynamic_slice_in_dim(v, t * WIDTH, WIDTH, 0)
        return jnp.broadcast_to(mine[:, None], (WIDTH, TOK))

    vmem = pl.BlockSpec(memory_space=pltpu.VMEM)
    hbm = pl.BlockSpec(memory_space=pl.ANY)
    piece = (WIDTH, TOK)
    whole = (D, TOK)
    wg, bg, codes = pl.pallas_call(
        body,
        out_shape=(
            jax.ShapeDtypeStruct((WIDTH, LANES), BF16),
            jax.ShapeDtypeStruct((1, LANES), F32),
            jax.ShapeDtypeStruct((TOK, LANES), BF16),
        ),
        in_specs=[vmem] * 5 + [hbm] * 5 + [vmem] * 3,
        out_specs=(hbm, hbm, hbm),
        scratch_shapes=[
            pltpu.VMEM((D, 256), BF16),
            pltpu.VMEM((D, 128), BF16),
            pltpu.VMEM((D, 128), BF16),
            pltpu.VMEM((256, D), BF16),
            pltpu.VMEM((D, LANES), BF16),
            pltpu.VMEM(whole, BF16),
            pltpu.VMEM((TOK, D), BF16),
            pltpu.VMEM(whole, BF16),
            pltpu.VMEM((8, *piece), BF16),
            pltpu.VMEM((8, *piece), BF16),
            pltpu.VMEM((8, *piece), BF16),
            pltpu.VMEM(whole, BF16),
            pltpu.VMEM((8, *piece), BF16),
            pltpu.VMEM((8, *piece), BF16),
            pltpu.VMEM((8, *piece), BF16),
            pltpu.VMEM((TOK, TOK), jnp.int32),
            pltpu.VMEM((TOK, TOK), F32),
            pltpu.VMEM((GROUPS, 16, 256), BF16),
            pltpu.VMEM((GROUPS, 16, 256), BF16),
            pltpu.VMEM(whole, BF16),
            pltpu.VMEM(whole, BF16),
            pltpu.VMEM(piece, BF16),
            pltpu.VMEM(piece, BF16),
            pltpu.VMEM(piece, BF16),
            pltpu.VMEM(piece, BF16),
            pltpu.VMEM(whole, BF16),
            pltpu.VMEM(whole, BF16),
            pltpu.VMEM((TOK, LANES), F32),
            pltpu.VMEM((TOK, LANES), F32),
            pltpu.VMEM((TOKENS, LANES), BF16),
            pltpu.VMEM((TOKENS, LANES), BF16),
            pltpu.VMEM((WIDTH, LANES), F32),
            pltpu.VMEM((WIDTH, LANES), BF16),
            pltpu.VMEM((1, LANES), F32),
            pltpu.SemaphoreType.DMA((8,)),
            pltpu.SemaphoreType.DMA((SEMS,)),
            pltpu.SemaphoreType.DMA((SEMS,)),
        ],
        compiler_params=pltpu.CompilerParams(
            collective_id=0, has_side_effects=True, vmem_limit_bytes=60 * 1024 * 1024
        ),
    )(
        residual.T,
        segments,
        row_perm.reshape(1, TOK),
        pre_gain.reshape(1, D),
        column(post_gain),
        w_query,
        w_key,
        w_value,
        w_out,
        sae_weight,
        enc_bias.reshape(1, LANES),
        thresholds.reshape(1, LANES),
        column(dec_bias),
    )
    return wg, bg.reshape(LANES), codes


def solution(mesh):
    features = ("tensor", "latent")
    return jax.shard_map(
        local,
        mesh=mesh,
        in_specs=(
            P("dp", features),
            P("dp", None),
            P("dp"),
            P(),
            P(),
            P(None, features),
            P(None, features),
            P(None, features),
            P(features, None),
            P("dp", features),
            P(features),
            P(features),
            P(),
        ),
        out_specs=(P("dp", features), P(features), P("dp", features)),
        check_vma=False,
    )
```

time: 523 us -> 243 us (0.46)
  waiting for transfers between devices: 381 us -> 0 us
  Pallas kernels: 0 us -> 233 us
  matrix products: 45.7 us -> 0 us
  blocking collectives: 29 us -> 0 us
  starting transfers between devices: 26.3 us -> 0 us
  between operations: 14 us -> 0.65 us
  other arithmetic: 12.1 us -> 0 us
    all_gather x4 -> x0, waiting for transfers between devices: 245 us -> none  [the longest x1 112 us: local(): weights = lax.all_gather(sae_weight, 'dp', axis=0, tiled=True)]
    pallas_call x0 -> x1, Pallas kernels: none -> 233 us  [local(): pl.pallas_call(body, out_shape=(jax.ShapeDtypeStruct((WIDTH, LANES), BF16...]
    reduce_scatter x1 -> x0, waiting for transfers between devices: 95.9 us -> none  [local(): lax.psum_scatter((grad_scale * (leading_summand + second_term)).astype(jn...]
    dot_general x10 -> x0, matrix products: 45.7 us -> none  [the longest x1 10.7 us: local(): lax.dot_general(error_bf, latent_acts, contract_first, preferred_element_...]
    all_to_all x4 -> x0, waiting for transfers between devices: 38.5 us -> none  [the longest x2 32.3 us: sum_at_owner(): tiles = lax.all_to_all(split_up(array, dim, size), axis, 0, 0, tiled=True)]
    all_to_all x2 -> x0, blocking collectives: 29 us -> none  [the longest x1 15 us: local(): lax.all_to_all(hidden[wanted], 'dp', split_axis=0, concat_axis=0, tiled=T...]
    all_to_all x4 -> x0, starting transfers between devices: 25.9 us -> none  [the longest x2 11 us: sum_at_owner(): tiles = lax.all_to_all(split_up(array, dim, size), axis, 0, 0, tiled=True)]
  transfers between devices with their start and end apart: 9 -> 0, of which waited for: 8 -> 0; matrix products, arithmetic and copies ran while one was open for 6% -> 0% of each run, Pallas kernels for 0% -> 0%
where the time goes in v1:
time: 243 us
  Pallas kernels  233 us (96%)
  local copies, waits for them, and re-layouts  9.28 us (4%)
    pallas_call x1, Pallas kernels, local(): pl.pallas_call(body, out_shape=(jax.ShapeDtypeStruct((WIDTH, LANES), BF16...  233 us

profile of v1, /device:TPU:1, one launch (start us, length us, event | category | flops | bytes accessed | tf_op | source)
XLA Modules:
  0.0 243.0 jit_solution(7474015614126415054)
XLA Ops:
  0.6 0.8 dynamic_slice.6
  1.4 0.8 dynamic_slice.7
  2.2 1.4 reshape.24.pre_gain
  3.5 0.8 broadcast_in_dim.5.bias_col
  4.3 0.8 broadcast_in_dim.4.gain_col
  5.1 233.1 %shard_map.148 = (bf16[288,1024]{1,0:T(8,128)(2,1)}, f32[1,1024]{1,0:T(1,128)}, bf16[128,1024]{1,0:T(8,128)(2,1)}) custom-call(bf16[288,128]{1,0:T(8,128)(2,1)} %bitcast.5, s32[1,128]{1,0:T(1,128)} %seg.1, s32[1,128]{1,0:T(1,128)} %bitcast.9, f32[1,4608]{1,0:T(1,128)} %reshape.24.pre_gain, f32[288,128]{1,0:T(8,128)} %broadcast_in_dim.4.gain_col, ...), custom_call_target="tpu_custom_call" | custom-call | tf_op jit(solution)/shard_map/pallas_call | solution.py:580
  238.1 1.9 copy.19
  240.1 1.3 copy.20
  241.3 1.7 copy.21

commit v2 on v1

v2 whole, which is shorter than its diff:
```python
import math

import jax
import jax.numpy as jnp
from jax import lax
from jax.experimental import pallas as pl
from jax.experimental.pallas import tpu as pltpu
from jax.sharding import PartitionSpec as P

D = 4608
HEADS = 32
HEAD = 128
LANES = 1024
TOK = 128
GROUPS = 16
TOKENS = TOK * GROUPS
BLOCK = 8
WIDTH = D // 16
HALF = D // 2
PAIR = 2 * TOK
SEMS = 300

epsilon = 1e-06
softcap = 50.0
ramp_width = 0.05
rotary_base = 10000.0

MESH = pl.DeviceIdType.MESH
F32 = jnp.float32
BF16 = jnp.bfloat16
ROW_BY_ROW = (((1,), (1,)), ((), ()))


def dot(a, b):
    return jnp.dot(a, b, preferred_element_type=F32)


def dot_t(a, b):
    return lax.dot_general(a, b, ROW_BY_ROW, preferred_element_type=F32)


class Place:
    def __init__(self):
        self.dp = lax.axis_index("dp")
        self.ten = lax.axis_index("tensor")
        self.lat = lax.axis_index("latent")
        self.xl, self.z = self.dp // 8, self.dp % 8
        self.xh, self.core = self.ten // 2, self.ten % 2
        self.t = self.ten * 4 + self.lat
        self.eighth = self.core * 4 + self.lat
        self.half = (self.xl + self.xh) % 2
        self.group = (self.xl + self.xh + 1) % 2

    def at(self, dp=None, ten=None, lat=None):
        return {
            "dp": self.dp if dp is None else dp,
            "tensor": self.ten if ten is None else ten,
            "latent": self.lat if lat is None else lat,
        }

    def at_x(self):
        return self.at(dp=(1 - self.xl) * 8 + self.z)

    def chip(self, k, sign=1):
        return (self.xh + k // 4) % 2, (self.lat + sign * (k % 4) + 4) % 4

    def by_device(self, k, core, sign=1):
        xh, y = self.chip(k, sign)
        return (xh * 2 + core) * 4 + y

    def by_half(self, k, core, sign=1):
        xh, y = self.chip(k, sign)
        return (((self.xl + xh) % 2) * 2 + core) * 4 + y

    def by_group(self, k, core, sign=1):
        xh, y = self.chip(k, sign)
        return (((self.xl + xh + 1) % 2) * 2 + core) * 4 + y

    def peer(self, k, core=None):
        xh, y = self.chip(k)
        return self.at(ten=xh * 2 + (self.core if core is None else core), lat=y)

    def sibling(self):
        return self.at(ten=self.xh * 2 + 1 - self.core)


class Net:
    def __init__(self, send, recv):
        self.send, self.recv, self.used, self.open = send, recv, 0, []

    def copy(self, src, dst, device):
        i = self.used
        self.used += 1
        assert i < SEMS
        c = pltpu.make_async_remote_copy(
            src_ref=src,
            dst_ref=dst,
            send_sem=self.send.at[i],
            recv_sem=self.recv.at[i],
            device_id=device,
            device_id_type=MESH,
        )
        self.open.append(c)
        return c

    def close(self):
        for c in self.open:
            c.wait_send()
        self.open = []


FAR_FIRST = (6, 5, 7, 4, 2, 1, 3)
NEAR_FIRST = (1, 3, 2, 4, 5, 7, 6)


def piece_rows(ref, index):
    return ref.at[pl.ds(pl.multiple_of(index * WIDTH, 32), WIDTH)]


class Gather:
    def __init__(self, net, me, buf, piece):
        self.net, self.me, self.buf, self.piece = net, me, buf, piece

    def send(self, k, device):
        ref = piece_rows(self.buf, self.piece(k, self.me.core, -1))
        c = self.net.copy(ref, ref, device)
        c.start()
        return c

    def start(self):
        me = self.me
        self.first = {k: self.send(0, me.peer(k)) for k in (4, 2, 1, 3)}
        self.near = {0: self.send(0, me.sibling())}

    def finish(self):
        me = self.me
        self.first[4].wait_recv()
        second = {k: self.send(4, me.peer(k)) for k in (2, 1, 3)}
        self.near[4] = self.send(4, me.sibling())
        for k in (1, 3, 2):
            self.first[k].wait_recv()
            self.near[k] = self.send(k, me.sibling())
        for k in (1, 3, 2):
            second[k].wait_recv()
            self.near[4 + k] = self.send(4 + k, me.sibling())
        for c in self.near.values():
            c.wait_recv()


def reduce_to_owner(net, me, piece, part, mate, out, got):
    order = (*FAR_FIRST, 0)
    pair = {}
    for k in order:
        pair[k] = net.copy(piece_rows(part, piece(k, 1 - me.core)), mate.at[k], me.sibling())
        pair[k].start()
    away = {}
    for k in order:
        pair[k].wait_recv()
        both = piece_rows(part, piece(k, me.core))[...].astype(F32) + mate[k].astype(F32)
        if k == 0:
            total = both
        else:
            out[k] = both.astype(BF16)
            away[k] = net.copy(out.at[k], got.at[k], me.peer(k))
            away[k].start()
    for k in NEAR_FIRST:
        away[k].wait_recv()
        total = total + got[k].astype(F32)
    return total


class Ring:
    def __init__(self, net, me, buf, size, width):
        self.net, self.me, self.buf, self.size, self.width = net, me, buf, size, width
        self.moves = {}

    def move(self, chunk, sign, step):
        me = self.me
        lo, count = 0, self.size
        if step == 4:
            count = self.size // 2
            lo = 0 if sign > 0 else count
        block = (me.z - sign * (step - 1) + 8) % 8
        ref = self.buf.at[
            pl.ds(pl.multiple_of(block * self.size + lo, 16), count),
            pl.ds(chunk * self.width, self.width),
        ]
        c = self.net.copy(ref, ref, me.at(dp=me.xl * 8 + (me.z + sign + 8) % 8))
        c.start()
        self.moves[chunk, sign, step] = c

    def start(self, chunk):
        for sign in (1, -1):
            self.move(chunk, sign, 1)

    def tick(self, chunk, step):
        for sign in (1, -1):
            self.moves[chunk, sign, step].wait_recv()
            if step < 4:
                self.move(chunk, sign, step + 1)


def transpose_into(src, dst, count):
    @pl.loop(0, count)
    def _(i):
        at = pl.multiple_of(i * TOK, TOK)
        dst[:, pl.ds(at, TOK)] = src[pl.ds(at, TOK), :].T


def transpose_pair(src, dst):
    @pl.loop(0, HALF // TOK)
    def _(i):
        at = pl.multiple_of(i * TOK, TOK)
        dst[:TOK, pl.ds(at, TOK)] = src[pl.ds(at, TOK), :].T
        dst[TOK:, pl.ds(at, TOK)] = src[pl.ds(HALF + at, TOK), :].T


def body(
    res,
    seg,
    perm,
    pre_gain,
    gain_col,
    wq_hbm,
    wk_hbm,
    wv_hbm,
    wo_hbm,
    w_hbm,
    enc_bias,
    thr,
    bias_col,
    wg_out,
    bg_out,
    codes_out,
    wq,
    wk,
    wv,
    wo,
    w,
    feat,
    rows,
    part,
    mate,
    out,
    got,
    part2,
    mate2,
    out2,
    got2,
    asked,
    squares,
    sent,
    taken,
    sae_f,
    err_f,
    sae_mine,
    err_mine,
    turned_s,
    turned_e,
    sae_t,
    err_t,
    pair_rows,
    acts_here,
    acts_there,
    slope,
    codes2,
    both,
    grad_sent,
    grad_got,
    codes,
    grads,
    left_s,
    left_e,
    wg,
    wg_sent,
    wg_got,
    final,
    bg_here,
    bg_there,
    bg,
    local_sem,
    send_sem,
    recv_sem,
):
    me = Place()
    net = Net(send_sem, recv_sem)

    loads = []
    for i, (src, dst) in enumerate(
        [
            (w_hbm, piece_rows(w, me.z)),
            (wq_hbm, wq),
            (wk_hbm, wk),
            (wv_hbm, wv),
            (wo_hbm, wo),
        ]
    ):
        loads.append(pltpu.make_async_copy(src, dst, local_sem.at[i]))
        loads[-1].start()

    turn = (me.z + 1) % 8
    turn_to = me.at(dp=me.group * 8 + me.eighth, ten=me.xl * 2 + turn // 4, lat=turn % 4)
    turn_from = me.at(dp=me.xh * 8 + (me.eighth + 7) % 8, ten=me.group * 2 + me.z // 4, lat=me.z % 4)

    greeted = [turn_from, me.sibling()]
    for k in range(1, 8):
        for core in range(2):
            greeted.append(me.peer(k, core))

    def dp_peer(j):
        return ((me.xl + j // 8) % 2) * 8 + (me.z + j % 8) % 8

    for j in range(1, 16):
        greeted.append(me.at(dp=dp_peer(j)))
    for j in range(16):
        if j != 8:
            x = (me.group + j // 8) % 2
            z = (me.z + 8 - j % 8) % 8
            greeted.append(me.at(dp=x * 8 + z, ten=((x + me.xl) % 2) * 2 + me.core))
    barrier = pltpu.get_barrier_semaphore()
    for device in greeted:
        pl.semaphore_signal(barrier, inc=1, device_id=device, device_id_type=MESH)

    @pl.when(me.xh == 1)
    def _():
        pl.semaphore_signal(barrier, inc=1, device_id=me.at_x(), device_id_type=MESH)

    pl.semaphore_wait(barrier, len(greeted) + me.xh)

    piece_rows(feat, me.t)[...] = res[...]
    gather = Gather(net, me, feat, me.by_device)
    gather.start()

    def eight_rows(ref, index):
        return ref.at[pl.ds(pl.multiple_of(index * 8, 8), 8)]

    eight_rows(asked, me.dp)[...] = jnp.broadcast_to(perm[...], (8, TOK))
    asks = []
    for j in range(1, 16):
        own = eight_rows(asked, me.dp)
        asks.append(net.copy(own, own, me.at(dp=dp_peer(j))))
        asks[-1].start()

    loads[0].wait()
    ring = Ring(net, me, w, WIDTH, 512)
    ring.start(0)
    ring.start(1)

    lane = lax.broadcasted_iota(jnp.int32, (TOK, TOK), 1)
    row = lax.broadcasted_iota(jnp.int32, (TOK, TOK), 0)
    seg_k = jnp.broadcast_to(seg[...].astype(F32), (TOK, TOK))
    same = seg_k == seg_k.T
    position = jnp.sum(jnp.where(same & (lane < row), 1.0, 0.0), axis=1, keepdims=True)
    allowed = same & (lane <= row)
    step = (lane % 64).astype(F32)
    angle = position * jnp.exp(step * (-2.0 / HEAD * math.log(rotary_base)))
    cosine = jnp.cos(angle)
    sine = jnp.sin(angle)
    sine = jnp.where(lane < 64, -sine, sine)

    for c in asks:
        c.wait_recv()
    place = 8 * me.dp + row % 8
    mine = jnp.where(lane == place, asked[...], 0).astype(F32)
    number = jnp.sum(mine, axis=1, keepdims=True) - (me.dp * TOK).astype(F32)
    pick = jnp.where(number == lane.astype(F32), 1.0, 0.0).astype(BF16)

    gather.finish()
    ring.tick(0, 1)
    transpose_into(feat, rows, D // TOK)

    def add_squares(i, acc):
        x = rows[:, pl.ds(pl.multiple_of(i * TOK, TOK), TOK)].astype(F32)
        return acc + x * x

    acc = lax.fori_loop(0, D // TOK, add_squares, jnp.zeros((TOK, TOK), F32), unroll=4)
    scale = lax.rsqrt(jnp.sum(acc, axis=1, keepdims=True) * (1.0 / D) + epsilon)

    @pl.loop(0, D // TOK, unroll=4)
    def _(i):
        at = pl.ds(pl.multiple_of(i * TOK, TOK), TOK)
        rows[:, at] = (rows[:, at].astype(F32) * scale * pre_gain[:, at]).astype(BF16)

    for c in loads[1:]:
        c.wait()
    normed = rows[...]
    query = dot(normed, wq[...])
    key = dot(normed, wk[...])
    value = dot(normed, wv[...]).astype(BF16)

    def rotate(v):
        return (v * cosine + pltpu.roll(v, 64, 1) * sine).astype(BF16)

    key = rotate(key)
    heads = []
    for h in range(2):
        q = rotate(query[:, h * HEAD : (h + 1) * HEAD])
        scores = dot_t(q, key) * (D / HEADS) ** (-0.5)
        scores = softcap * jnp.tanh(scores / softcap)
        weighted = jnp.where(allowed, jnp.exp(scores), 0.0)
        probs = (weighted / jnp.sum(weighted, axis=1, keepdims=True)).astype(BF16)
        heads.append(dot(probs, value).astype(BF16))
    heads = jnp.concatenate(heads, axis=1)

    ring.tick(1, 1)

    @pl.loop(0, D // 256)
    def _(i):
        at = pl.multiple_of(i * 256, 256)
        part[pl.ds(at, 256), :] = dot(heads, wo[:, pl.ds(at, 256)]).astype(BF16).T

    attn = reduce_to_owner(net, me, me.by_half, part, mate, out, got)

    total = jnp.sum(attn * attn, axis=0, keepdims=True)
    own = eight_rows(squares, me.t)
    own[...] = jnp.broadcast_to(total, (8, TOK))
    sums = []
    for k in range(8):
        for core in range(2):
            if k or core:
                device = me.peer(k, (me.core + core) % 2)
                sums.append(net.copy(own, own, device))
                sums[-1].start()
    ring.tick(0, 2)
    for c in sums:
        c.wait_recv()
    ring.tick(1, 2)
    total = jnp.sum(squares[...], axis=0, keepdims=True) * (0.125 / D)
    stream = piece_rows(feat, me.half * 8 + me.eighth)[...].astype(F32)
    hidden = stream + attn * lax.rsqrt(total + epsilon) * gain_col[...]
    hidden = hidden.astype(BF16)

    low = dot_t(pick, hidden[:256])
    high = dot_t(pick, hidden[32:])
    for g in range(GROUPS):
        block = jnp.concatenate([low[8 * g : 8 * g + 8], high[8 * g : 8 * g + 8]], axis=0)
        sent[g] = block.astype(BF16)
    moves = []
    to = dp_peer(8)
    other = net.copy(sent.at[to], taken.at[me.dp], me.at_x())
    net.open.pop()

    @pl.when(me.xh == 1)
    def _():
        other.start()

    @pl.when(me.xh == 0)
    def _():
        taken[me.dp] = sent[to]

    for j in (15, 14, 13, 12, 11, 10, 9, 4, 3, 5, 2, 6, 1, 7, 0):
        to = dp_peer(j)
        x, z = to // 8, to % 8
        ten = ((x + me.half + 1) % 2) * 2 + me.core
        moves.append(net.copy(sent.at[to], taken.at[me.dp], me.at(dp=me.half * 8 + z, ten=ten)))
        moves[-1].start()

    @pl.when(me.xh == 1)
    def _():
        other.wait()

    for c in moves:
        c.wait_recv()
    low, high = [], []
    for g in range(GROUPS):
        block = taken[g].astype(F32)
        low.append(block[:8])
        high.append(block[8:, 128:])
    low = jnp.concatenate(low, axis=0)
    high = jnp.concatenate(high, axis=0)
    sae_mine[...] = jnp.concatenate([low.T, high.T[96:]], axis=0).astype(BF16)
    piece_rows(sae_f, me.group * 8 + me.eighth)[...] = sae_mine[...]
    gather = Gather(net, me, sae_f, me.by_group)
    gather.start()
    ring.tick(0, 3)
    ring.tick(1, 3)
    gather.finish()
    turn_s = net.copy(sae_mine, turned_s, turn_to)
    turn_s.start()
    transpose_pair(sae_f, pair_rows)
    ring.tick(0, 4)
    ring.tick(1, 4)

    swaps = []
    for n in range(4):
        at = slice(256 * n, 256 * n + 256)
        acts_here[n] = dot(pair_rows[...], w[:, at]).astype(BF16)
        swaps.append(net.copy(acts_here.at[n], acts_there.at[n], me.at_x()))
        swaps[-1].start()
    turn_s.wait_recv()
    piece_rows(sae_t, me.t)[...] = turned_s[...]
    gather_st = Gather(net, me, sae_t, me.by_device)
    for n in range(4):
        at = slice(256 * n, 256 * n + 256)
        swaps[n].wait_recv()
        acts = acts_here[n].astype(F32) + acts_there[n].astype(F32) + enc_bias[:, at]
        opened = jax.nn.sigmoid((acts - thr[:, at]) / ramp_width)
        slope[:, at] = opened + acts * opened * (1.0 - opened) / ramp_width
        codes2[:, at] = (acts * opened).astype(BF16)
    my_rows = pl.ds(pl.multiple_of(me.xl * TOK, TOK), TOK)
    my_block = pl.ds(pl.multiple_of(me.z * TOK, TOK), TOK)
    codes[my_block, :] = codes2[my_rows, :]
    ring_c = Ring(net, me, codes, TOK, 512)
    ring_c.start(0)
    ring_c.start(1)
    save_codes = pltpu.make_async_copy(codes.at[my_block], codes_out, local_sem.at[5])
    save_codes.start()
    mine = codes2[...]

    @pl.loop(0, 8)
    def _(i):
        at = pl.ds(pl.multiple_of(i * WIDTH, 32), WIDTH)
        rebuilt = dot_t(w[at, :], mine).astype(BF16)
        part2[at, :] = rebuilt[:, :TOK]
        part2[pl.ds(pl.multiple_of(HALF + i * WIDTH, 32), WIDTH), :] = rebuilt[:, TOK:]

    rebuilt = reduce_to_owner(net, me, me.by_group, part2, mate2, out2, got2)
    error = (rebuilt + bias_col[...] - sae_mine[...].astype(F32)).astype(BF16)
    err_mine[...] = error
    piece_rows(err_f, me.group * 8 + me.eighth)[...] = error
    gather = Gather(net, me, err_f, me.by_group)
    gather.start()
    ring_c.tick(0, 1)
    ring_c.tick(1, 1)
    gather.finish()
    turn_e = net.copy(err_mine, turned_e, turn_to)
    turn_e.start()
    gather_st.start()
    transpose_pair(err_f, pair_rows)
    swaps = []
    mates_rows = pl.ds(pl.multiple_of((1 - me.xl) * TOK, TOK), TOK)
    for n in range(4):
        both[n] = dot(pair_rows[...], w[:, 256 * n : 256 * n + 256])
        grad_sent[n] = both[n, mates_rows, :].astype(BF16)
        swaps.append(net.copy(grad_sent.at[n], grad_got.at[n], me.at_x()))
        swaps[-1].start()
        if n == 0:
            ring_c.tick(0, 2)
        if n == 1:
            ring_c.tick(1, 2)
    ring_g = Ring(net, me, grads, TOK, 256)

    def finish_grads(n):
        at = slice(256 * n, 256 * n + 256)
        swaps[n].wait_recv()
        product = both[n, my_rows, :] + grad_got[n].astype(F32)
        grads[my_block, at] = (product * slope[my_rows, at]).astype(BF16)

    for n in range(4):
        finish_grads(n)
        if n < 2:
            ring_g.start(n)
    ring_c.tick(0, 3)
    ring_c.tick(1, 3)
    ring_g.tick(0, 1)
    turn_e.wait_recv()
    piece_rows(err_t, me.t)[...] = turned_e[...]
    gather_et = Gather(net, me, err_t, me.by_device)
    gather_et.start()
    gather_st.finish()
    ring_g.tick(1, 1)
    ring_c.tick(0, 4)
    ring_c.tick(1, 4)
    gather_et.finish()
    ring_g.tick(0, 2)

    def side_by_side(src, dst):
        for f in range(2):
            for z in range(8):
                at = (f * 8 + (z + 1) % 8) * WIDTH
                dst[f, :, z * TOK : (z + 1) * TOK] = src[at : at + WIDTH, :]

    side_by_side(sae_t, left_s)
    side_by_side(err_t, left_e)
    for f in range(2):
        for n in range(4):
            at = slice(256 * n, 256 * n + 256)
            wg[f, :, at] = dot(left_e[f], codes[:, at])

    grad_scale = 1.0 / math.sqrt(TOKENS)
    ones = jnp.ones((8, 8 * TOK), BF16)
    swaps = []

    def finish_columns(n):
        at = slice(256 * n, 256 * n + 256)
        mates = 1 - me.xl
        table = grads[:, at]
        theirs = wg[mates, :, at] + dot(left_s[mates], table)
        wg_sent[n] = (theirs * grad_scale).astype(BF16)
        swaps.append(net.copy(wg_sent.at[n], wg_got.at[n], me.at_x()))
        swaps[-1].start()
        wg[me.xl, :, at] += dot(left_s[me.xl], table)
        bg_here[:, at] = dot(ones, table)

    def save_columns(n):
        at = slice(256 * n, 256 * n + 256)
        swaps[n].wait_recv()
        final[:, at] = (wg[me.xl, :, at] * grad_scale + wg_got[n].astype(F32)).astype(BF16)

    ring_g.tick(1, 2)
    ring_g.tick(0, 3)
    ring_g.start(2)
    ring_g.tick(1, 3)
    ring_g.start(3)
    ring_g.tick(0, 4)
    ring_g.tick(2, 1)
    finish_columns(0)
    ring_g.tick(1, 4)
    ring_g.tick(3, 1)
    finish_columns(1)
    ring_g.tick(2, 2)
    ring_g.tick(3, 2)
    save_columns(0)
    ring_g.tick(2, 3)
    ring_g.tick(3, 3)
    ring_g.tick(2, 4)
    finish_columns(2)
    ring_g.tick(3, 4)
    finish_columns(3)
    bias_swap = net.copy(bg_here, bg_there, me.at_x())
    bias_swap.start()
    save_columns(1)
    save_columns(2)
    save_columns(3)
    save_wg = pltpu.make_async_copy(final, wg_out, local_sem.at[6])
    save_wg.start()
    bias_swap.wait_recv()
    bg[...] = grad_scale * (bg_here[0:1, :] + bg_there[0:1, :])
    save_bg = pltpu.make_async_copy(bg, bg_out, local_sem.at[7])
    save_bg.start()
    net.close()
    save_codes.wait()
    save_wg.wait()
    save_bg.wait()


def local(
    residual,
    segments,
    row_perm,
    pre_gain,
    post_gain,
    w_query,
    w_key,
    w_value,
    w_out,
    sae_weight,
    enc_bias,
    thresholds,
    dec_bias,
):
    x, core_y = lax.axis_index("dp") // 8, lax.axis_index(("tensor", "latent"))
    half = (x + core_y // 8) % 2

    def column(v, half):
        mine = lax.dynamic_slice_in_dim(v, (half * 8 + core_y % 8) * WIDTH, WIDTH, 0)
        return jnp.broadcast_to(mine[:, None], (WIDTH, TOK))

    vmem = pl.BlockSpec(memory_space=pltpu.VMEM)
    hbm = pl.BlockSpec(memory_space=pl.ANY)
    piece = (WIDTH, TOK)
    whole = (D, TOK)
    wg, bg, codes = pl.pallas_call(
        body,
        out_shape=(
            jax.ShapeDtypeStruct((WIDTH, LANES), BF16),
            jax.ShapeDtypeStruct((1, LANES), F32),
            jax.ShapeDtypeStruct((TOK, LANES), BF16),
        ),
        in_specs=[vmem] * 5 + [hbm] * 5 + [vmem] * 3,
        out_specs=(hbm, hbm, hbm),
        scratch_shapes=[
            pltpu.VMEM((D, 256), BF16),
            pltpu.VMEM((D, 128), BF16),
            pltpu.VMEM((D, 128), BF16),
            pltpu.VMEM((256, D), BF16),
            pltpu.VMEM((HALF, LANES), BF16),
            pltpu.VMEM(whole, BF16),
            pltpu.VMEM((TOK, D), BF16),
            pltpu.VMEM(whole, BF16),
            pltpu.VMEM((8, *piece), BF16),
            pltpu.VMEM((8, *piece), BF16),
            pltpu.VMEM((8, *piece), BF16),
            pltpu.VMEM(whole, BF16),
            pltpu.VMEM((8, *piece), BF16),
            pltpu.VMEM((8, *piece), BF16),
            pltpu.VMEM((8, *piece), BF16),
            pltpu.VMEM((TOK, TOK), jnp.int32),
            pltpu.VMEM((TOK, TOK), F32),
            pltpu.VMEM((GROUPS, 16, 256), BF16),
            pltpu.VMEM((GROUPS, 16, 256), BF16),
            pltpu.VMEM(whole, BF16),
            pltpu.VMEM(whole, BF16),
            pltpu.VMEM(piece, BF16),
            pltpu.VMEM(piece, BF16),
            pltpu.VMEM(piece, BF16),
            pltpu.VMEM(piece, BF16),
            pltpu.VMEM(whole, BF16),
            pltpu.VMEM(whole, BF16),
            pltpu.VMEM((PAIR, HALF), BF16),
            pltpu.VMEM((4, PAIR, 256), BF16),
            pltpu.VMEM((4, PAIR, 256), BF16),
            pltpu.VMEM((PAIR, LANES), F32),
            pltpu.VMEM((PAIR, LANES), BF16),
            pltpu.VMEM((4, PAIR, 256), F32),
            pltpu.VMEM((4, TOK, 256), BF16),
            pltpu.VMEM((4, TOK, 256), BF16),
            pltpu.VMEM((8 * TOK, LANES), BF16),
            pltpu.VMEM((8 * TOK, LANES), BF16),
            pltpu.VMEM((2, WIDTH, 8 * TOK), BF16),
            pltpu.VMEM((2, WIDTH, 8 * TOK), BF16),
            pltpu.VMEM((2, WIDTH, LANES), F32),
            pltpu.VMEM((4, WIDTH, 256), BF16),
            pltpu.VMEM((4, WIDTH, 256), BF16),
            pltpu.VMEM((WIDTH, LANES), BF16),
            pltpu.VMEM((8, LANES), F32),
            pltpu.VMEM((8, LANES), F32),
            pltpu.VMEM((1, LANES), F32),
            pltpu.SemaphoreType.DMA((8,)),
            pltpu.SemaphoreType.DMA((SEMS,)),
            pltpu.SemaphoreType.DMA((SEMS,)),
        ],
        compiler_params=pltpu.CompilerParams(
            collective_id=0, has_side_effects=True, vmem_limit_bytes=60 * 1024 * 1024
        ),
    )(
        residual.T,
        segments,
        row_perm.reshape(1, TOK),
        pre_gain.reshape(1, D),
        column(post_gain, half),
        w_query,
        w_key,
        w_value,
        w_out,
        sae_weight,
        enc_bias.reshape(1, LANES),
        thresholds.reshape(1, LANES),
        column(dec_bias, x),
    )
    return wg, bg.reshape(LANES), codes


def solution(mesh):
    features = ("tensor", "latent")
    return jax.shard_map(
        local,
        mesh=mesh,
        in_specs=(
            P("dp", features),
            P("dp", None),
            P("dp"),
            P(),
            P(),
            P(None, features),
            P(None, features),
            P(None, features),
            P(features, None),
            P("dp", features),
            P(features),
            P(features),
            P(),
        ),
        out_specs=(P("dp", features), P(features), P("dp", features)),
        check_vma=False,
    )
```

time: 243 us -> 187 us (0.77); the launches traced: 243 us -> 184 us
  Pallas kernels: 233 us -> 174 us
    pallas_call x1, Pallas kernels: 233 us -> 174 us  [local(): pl.pallas_call(body, out_shape=(jax.ShapeDtypeStruct((WIDTH, LANES), BF16...]
where the time goes in v2:
time: 187 us; the launch traced here: 184 us
  Pallas kernels  174 us (93%)
  local copies, waits for them, and re-layouts  9.28 us (5%)
    pallas_call x1, Pallas kernels, local(): pl.pallas_call(body, out_shape=(jax.ShapeDtypeStruct((WIDTH, LANES), BF16...  174 us
    unnamed x3, local copies, waits for them, and re-layouts  4.85 us

profile of v2, /device:TPU:1, one launch (start us, length us, event | category | flops | bytes accessed | tf_op | source)
XLA Modules:
  0.0 184.0 jit_solution(7317332062366511381)
XLA Ops:
  0.7 0.8 dynamic_slice.6
  1.5 0.8 dynamic_slice.7
  2.2 1.4 reshape.24.pre_gain
  3.6 0.8 broadcast_in_dim.5.bias_col
  4.4 0.8 broadcast_in_dim.4.gain_col
  5.1 174.1 %shard_map.148 = (bf16[288,1024]{1,0:T(8,128)(2,1)}, f32[1,1024]{1,0:T(1,128)}, bf16[128,1024]{1,0:T(8,128)(2,1)}) custom-call(bf16[288,128]{1,0:T(8,128)(2,1)} %bitcast.5, s32[1,128]{1,0:T(1,128)} %seg.1, s32[1,128]{1,0:T(1,128)} %bitcast.9, f32[1,4608]{1,0:T(1,128)} %reshape.24.pre_gain, f32[288,128]{1,0:T(8,128)} %broadcast_in_dim.4.gain_col, ...), custom_call_target="tpu_custom_call" | custom-call | tf_op jit(solution)/shard_map/pallas_call | solution.py:663
  179.2 1.9 %copy.19 = bf16[288,1024]{1,0:T(8,128)(2,1)} copy(bf16[288,1024]{1,0:T(8,128)(2,1)} %get-tuple-element.12) | data formatting | bytes 1179648
  181.1 1.3 copy.20
  182.4 1.7 copy.21

commit v3 on v2

--- a/solution.py
+++ b/solution.py
@@ -200,6 +200,13 @@
                 self.move(chunk, sign, step + 1)
 
 
+def spread(vec, piece, col):
+    for i in range(3):
+        row = vec[pl.ds(piece * 9 // 4 + i, 1), :]
+        col[i * TOK : (i + 1) * TOK, :] = jnp.broadcast_to(row, (TOK, TOK)).T
+    return pl.ds(pl.multiple_of(piece % 4 * 32, 32), WIDTH)
+
+
 def transpose_into(src, dst, count):
     @pl.loop(0, count)
     def _(i):
@@ -220,7 +227,7 @@
     seg,
     perm,
     pre_gain,
-    gain_col,
+    post_gain,
     wq_hbm,
     wk_hbm,
     wv_hbm,
@@ -228,7 +235,7 @@
     w_hbm,
     enc_bias,
     thr,
-    bias_col,
+    dec_bias,
     wg_out,
     bg_out,
     codes_out,
@@ -237,6 +244,8 @@
     wv,
     wo,
     w,
+    gain_col,
+    bias_col,
     feat,
     rows,
     part,
@@ -358,6 +367,9 @@
     sine = jnp.sin(angle)
     sine = jnp.where(lane < 64, -sine, sine)
 
+    gain_at = spread(post_gain, me.half * 8 + me.eighth, gain_col)
+    bias_at = spread(dec_bias, me.xl * 8 + me.eighth, bias_col)
+
     for c in asks:
         c.wait_recv()
     place = 8 * me.dp + row % 8
@@ -379,7 +391,7 @@
     @pl.loop(0, D // TOK, unroll=4)
     def _(i):
         at = pl.ds(pl.multiple_of(i * TOK, TOK), TOK)
-        rows[:, at] = (rows[:, at].astype(F32) * scale * pre_gain[:, at]).astype(BF16)
+        rows[:, at] = (rows[:, at].astype(F32) * scale * pre_gain[pl.ds(i, 1), :]).astype(BF16)
 
     for c in loads[1:]:
         c.wait()
@@ -427,7 +439,7 @@
     ring.tick(1, 2)
     total = jnp.sum(squares[...], axis=0, keepdims=True) * (0.125 / D)
     stream = piece_rows(feat, me.half * 8 + me.eighth)[...].astype(F32)
-    hidden = stream + attn * lax.rsqrt(total + epsilon) * gain_col[...]
+    hidden = stream + attn * lax.rsqrt(total + epsilon) * gain_col[gain_at, :]
     hidden = hidden.astype(BF16)
 
     low = dot_t(pick, hidden[:256])
@@ -490,6 +502,7 @@
     turn_s.wait_recv()
     piece_rows(sae_t, me.t)[...] = turned_s[...]
     gather_st = Gather(net, me, sae_t, me.by_device)
+    gather_st.start()
     for n in range(4):
         at = slice(256 * n, 256 * n + 256)
         swaps[n].wait_recv()
@@ -514,18 +527,24 @@
         part2[at, :] = rebuilt[:, :TOK]
         part2[pl.ds(pl.multiple_of(HALF + i * WIDTH, 32), WIDTH), :] = rebuilt[:, TOK:]
 
+    gather_st.finish()
+    ring_c.tick(0, 1)
+    ring_c.tick(1, 1)
     rebuilt = reduce_to_owner(net, me, me.by_group, part2, mate2, out2, got2)
-    error = (rebuilt + bias_col[...] - sae_mine[...].astype(F32)).astype(BF16)
+    error = (rebuilt + bias_col[bias_at, :] - sae_mine[...].astype(F32)).astype(BF16)
     err_mine[...] = error
     piece_rows(err_f, me.group * 8 + me.eighth)[...] = error
     gather = Gather(net, me, err_f, me.by_group)
     gather.start()
-    ring_c.tick(0, 1)
-    ring_c.tick(1, 1)
-    gather.finish()
     turn_e = net.copy(err_mine, turned_e, turn_to)
     turn_e.start()
-    gather_st.start()
+    ring_c.tick(0, 2)
+    ring_c.tick(1, 2)
+    gather.finish()
+    ring_c.tick(0, 3)
+    ring_c.tick(1, 3)
+    turn_e.wait_recv()
+    piece_rows(err_t, me.t)[...] = turned_e[...]
     transpose_pair(err_f, pair_rows)
     swaps = []
     mates_rows = pl.ds(pl.multiple_of((1 - me.xl) * TOK, TOK), TOK)
@@ -534,10 +553,6 @@
         grad_sent[n] = both[n, mates_rows, :].astype(BF16)
         swaps.append(net.copy(grad_sent.at[n], grad_got.at[n], me.at_x()))
         swaps[-1].start()
-        if n == 0:
-            ring_c.tick(0, 2)
-        if n == 1:
-            ring_c.tick(1, 2)
     ring_g = Ring(net, me, grads, TOK, 256)
 
     def finish_grads(n):
@@ -550,19 +565,12 @@
         finish_grads(n)
         if n < 2:
             ring_g.start(n)
-    ring_c.tick(0, 3)
-    ring_c.tick(1, 3)
-    ring_g.tick(0, 1)
-    turn_e.wait_recv()
-    piece_rows(err_t, me.t)[...] = turned_e[...]
     gather_et = Gather(net, me, err_t, me.by_device)
     gather_et.start()
-    gather_st.finish()
-    ring_g.tick(1, 1)
     ring_c.tick(0, 4)
     ring_c.tick(1, 4)
-    gather_et.finish()
-    ring_g.tick(0, 2)
+    ring_g.tick(0, 1)
+    ring_g.tick(1, 1)
 
     def side_by_side(src, dst):
         for f in range(2):
@@ -571,11 +579,22 @@
                 dst[f, :, z * TOK : (z + 1) * TOK] = src[at : at + WIDTH, :]
 
     side_by_side(sae_t, left_s)
+    ring_g.tick(0, 2)
+    ring_g.tick(1, 2)
+    ring_g.start(2)
+    gather_et.finish()
+    ring_g.tick(0, 3)
+    ring_g.tick(1, 3)
+    ring_g.start(3)
     side_by_side(err_t, left_e)
-    for f in range(2):
-        for n in range(4):
+
+    def error_term(n):
+        for f in range(2):
             at = slice(256 * n, 256 * n + 256)
             wg[f, :, at] = dot(left_e[f], codes[:, at])
+
+    error_term(0)
+    error_term(1)
 
     grad_scale = 1.0 / math.sqrt(TOKENS)
     ones = jnp.ones((8, 8 * TOK), BF16)
@@ -597,22 +616,19 @@
         swaps[n].wait_recv()
         final[:, at] = (wg[me.xl, :, at] * grad_scale + wg_got[n].astype(F32)).astype(BF16)
 
-    ring_g.tick(1, 2)
-    ring_g.tick(0, 3)
-    ring_g.start(2)
-    ring_g.tick(1, 3)
-    ring_g.start(3)
+    ring_g.tick(2, 1)
     ring_g.tick(0, 4)
-    ring_g.tick(2, 1)
     finish_columns(0)
+    ring_g.tick(3, 1)
     ring_g.tick(1, 4)
-    ring_g.tick(3, 1)
+    ring_g.tick(2, 2)
     finish_columns(1)
-    ring_g.tick(2, 2)
     ring_g.tick(3, 2)
+    error_term(2)
+    ring_g.tick(2, 3)
+    error_term(3)
+    ring_g.tick(3, 3)
     save_columns(0)
-    ring_g.tick(2, 3)
-    ring_g.tick(3, 3)
     ring_g.tick(2, 4)
     finish_columns(2)
     ring_g.tick(3, 4)
@@ -649,13 +665,6 @@
     thresholds,
     dec_bias,
 ):
-    x, core_y = lax.axis_index("dp") // 8, lax.axis_index(("tensor", "latent"))
-    half = (x + core_y // 8) % 2
-
-    def column(v, half):
-        mine = lax.dynamic_slice_in_dim(v, (half * 8 + core_y % 8) * WIDTH, WIDTH, 0)
-        return jnp.broadcast_to(mine[:, None], (WIDTH, TOK))
-
     vmem = pl.BlockSpec(memory_space=pltpu.VMEM)
     hbm = pl.BlockSpec(memory_space=pl.ANY)
     piece = (WIDTH, TOK)
@@ -675,6 +684,8 @@
             pltpu.VMEM((D, 128), BF16),
             pltpu.VMEM((256, D), BF16),
             pltpu.VMEM((HALF, LANES), BF16),
+            pltpu.VMEM((3 * TOK, TOK), F32),
+            pltpu.VMEM((3 * TOK, TOK), F32),
             pltpu.VMEM(whole, BF16),
             pltpu.VMEM((TOK, D), BF16),
             pltpu.VMEM(whole, BF16),
@@ -727,8 +738,8 @@
         residual.T,
         segments,
         row_perm.reshape(1, TOK),
-        pre_gain.reshape(1, D),
-        column(post_gain, half),
+        pre_gain.reshape(D // TOK, TOK),
+        post_gain.reshape(D // TOK, TOK),
         w_query,
         w_key,
         w_value,
@@ -736,7 +747,7 @@
         sae_weight,
         enc_bias.reshape(1, LANES),
         thresholds.reshape(1, LANES),
-        column(dec_bias, x),
+        dec_bias.reshape(D // TOK, TOK),
     )
     return wg, bg.reshape(LANES), codes
 

time: 187 us -> 179 us (0.957); the launches traced: 184 us -> 178 us
  local copies, waits for them, and re-layouts: 9.28 us -> 4.86 us
where the time goes in v3:
time: 179 us; the launch traced here: 178 us
  Pallas kernels  173 us (97%)
  local copies, waits for them, and re-layouts  4.86 us (3%)
    pallas_call x1, Pallas kernels, local(): pl.pallas_call(body, out_shape=(jax.ShapeDtypeStruct((WIDTH, LANES), BF16...  173 us
    unnamed x3, local copies, waits for them, and re-layouts  4.86 us

profile of v3, /device:TPU:1, one launch (start us, length us, event | category | flops | bytes accessed | tf_op | source)
XLA Modules:
  0.0 178.5 jit_solution(13632237497269071410)
XLA Ops:
  0.6 173.0 %shard_map.148 = (bf16[288,1024]{1,0:T(8,128)(2,1)}, f32[1,1024]{1,0:T(1,128)}, bf16[128,1024]{1,0:T(8,128)(2,1)}) custom-call(bf16[288,128]{1,0:T(8,128)(2,1)} %bitcast.8, s32[1,128]{1,0:T(1,128)} %seg.1, s32[1,128]{1,0:T(1,128)} %bitcast.15, f32[36,128]{1,0:T(8,128)} %bitcast.9, f32[36,128]{1,0:T(8,128)} %bitcast.10, bf16[4608,256]{1,0:T(8,128)(2,1)} %wq_hbm.1, ...), custom_call_target="tpu_custom_call" | custom-call | tf_op jit(solution)/shard_map/pallas_call | solution.py:672
  173.6 1.9 %copy.19 = bf16[288,1024]{1,0:T(8,128)(2,1)} copy(bf16[288,1024]{1,0:T(8,128)(2,1)} %get-tuple-element.12) | data formatting | bytes 1179648
  175.5 1.3 copy.20
  176.8 1.7 copy.21

commit v4 on v3

--- a/solution.py
+++ b/solution.py
@@ -563,14 +563,13 @@
 
     for n in range(4):
         finish_grads(n)
-        if n < 2:
-            ring_g.start(n)
+        ring_g.start(n)
     gather_et = Gather(net, me, err_t, me.by_device)
     gather_et.start()
     ring_c.tick(0, 4)
     ring_c.tick(1, 4)
-    ring_g.tick(0, 1)
-    ring_g.tick(1, 1)
+    for n in range(4):
+        ring_g.tick(n, 1)
 
     def side_by_side(src, dst):
         for f in range(2):
@@ -579,13 +578,10 @@
                 dst[f, :, z * TOK : (z + 1) * TOK] = src[at : at + WIDTH, :]
 
     side_by_side(sae_t, left_s)
+    gather_et.finish()
     ring_g.tick(0, 2)
     ring_g.tick(1, 2)
-    ring_g.start(2)
-    gather_et.finish()
-    ring_g.tick(0, 3)
-    ring_g.tick(1, 3)
-    ring_g.start(3)
+    ring_g.tick(2, 2)
     side_by_side(err_t, left_e)
 
     def error_term(n):
@@ -594,6 +590,9 @@
             wg[f, :, at] = dot(left_e[f], codes[:, at])
 
     error_term(0)
+    ring_g.tick(0, 3)
+    ring_g.tick(1, 3)
+    ring_g.tick(3, 2)
     error_term(1)
 
     grad_scale = 1.0 / math.sqrt(TOKENS)
@@ -616,18 +615,14 @@
         swaps[n].wait_recv()
         final[:, at] = (wg[me.xl, :, at] * grad_scale + wg_got[n].astype(F32)).astype(BF16)
 
-    ring_g.tick(2, 1)
     ring_g.tick(0, 4)
     finish_columns(0)
-    ring_g.tick(3, 1)
+    ring_g.tick(2, 3)
     ring_g.tick(1, 4)
-    ring_g.tick(2, 2)
     finish_columns(1)
-    ring_g.tick(3, 2)
+    ring_g.tick(3, 3)
     error_term(2)
-    ring_g.tick(2, 3)
     error_term(3)
-    ring_g.tick(3, 3)
     save_columns(0)
     ring_g.tick(2, 4)
     finish_columns(2)

time: 179 us -> 180 us (level)
  no operation moved by 1% of the time
where the time goes in v4:
time: 180 us; the launch traced here: 179 us
  Pallas kernels  173 us (96%)
  local copies, waits for them, and re-layouts  4.86 us (3%)
    pallas_call x1, Pallas kernels, local(): pl.pallas_call(body, out_shape=(jax.ShapeDtypeStruct((WIDTH, LANES), BF16...  173 us
    unnamed x3, local copies, waits for them, and re-layouts  4.86 us

profile of v4, /device:TPU:1, one launch (start us, length us, event | category | flops | bytes accessed | tf_op | source)
XLA Modules:
  0.0 178.6 jit_solution(10373494510471855767)
XLA Ops:
  0.6 173.1 %shard_map.148 = (bf16[288,1024]{1,0:T(8,128)(2,1)}, f32[1,1024]{1,0:T(1,128)}, bf16[128,1024]{1,0:T(8,128)(2,1)}) custom-call(bf16[288,128]{1,0:T(8,128)(2,1)} %bitcast.8, s32[1,128]{1,0:T(1,128)} %seg.1, s32[1,128]{1,0:T(1,128)} %bitcast.15, f32[36,128]{1,0:T(8,128)} %bitcast.9, f32[36,128]{1,0:T(8,128)} %bitcast.10, bf16[4608,256]{1,0:T(8,128)(2,1)} %wq_hbm.1, ...), custom_call_target="tpu_custom_call" | custom-call | tf_op jit(solution)/shard_map/pallas_call | solution.py:667
  173.7 1.9 %copy.19 = bf16[288,1024]{1,0:T(8,128)(2,1)} copy(bf16[288,1024]{1,0:T(8,128)(2,1)} %get-tuple-element.12) | data formatting | bytes 1179648
  175.6 1.3 copy.20
  176.9 1.7 copy.21

commit v5 on v3

--- a/solution.py
+++ b/solution.py
@@ -541,10 +541,6 @@
     ring_c.tick(0, 2)
     ring_c.tick(1, 2)
     gather.finish()
-    ring_c.tick(0, 3)
-    ring_c.tick(1, 3)
-    turn_e.wait_recv()
-    piece_rows(err_t, me.t)[...] = turned_e[...]
     transpose_pair(err_f, pair_rows)
     swaps = []
     mates_rows = pl.ds(pl.multiple_of((1 - me.xl) * TOK, TOK), TOK)
@@ -553,6 +549,12 @@
         grad_sent[n] = both[n, mates_rows, :].astype(BF16)
         swaps.append(net.copy(grad_sent.at[n], grad_got.at[n], me.at_x()))
         swaps[-1].start()
+    ring_c.tick(0, 3)
+    ring_c.tick(1, 3)
+    turn_e.wait_recv()
+    piece_rows(err_t, me.t)[...] = turned_e[...]
+    gather_et = Gather(net, me, err_t, me.by_device)
+    gather_et.start()
     ring_g = Ring(net, me, grads, TOK, 256)
 
     def finish_grads(n):
@@ -565,8 +567,6 @@
         finish_grads(n)
         if n < 2:
             ring_g.start(n)
-    gather_et = Gather(net, me, err_t, me.by_device)
-    gather_et.start()
     ring_c.tick(0, 4)
     ring_c.tick(1, 4)
     ring_g.tick(0, 1)

time: 179 us -> 181 us (1.011)
  no operation moved by 1% of the time
where the time goes in v5:
time: 181 us; the launch traced here: 179 us
  Pallas kernels  173 us (96%)
  local copies, waits for them, and re-layouts  4.86 us (3%)
    pallas_call x1, Pallas kernels, local(): pl.pallas_call(body, out_shape=(jax.ShapeDtypeStruct((WIDTH, LANES), BF16...  173 us
    unnamed x3, local copies, waits for them, and re-layouts  4.86 us

profile of v5, /device:TPU:1, one launch (start us, length us, event | category | flops | bytes accessed | tf_op | source)
XLA Modules:
  0.0 178.7 jit_solution(7983855890779996898)
XLA Ops:
  0.6 173.2 %shard_map.148 = (bf16[288,1024]{1,0:T(8,128)(2,1)}, f32[1,1024]{1,0:T(1,128)}, bf16[128,1024]{1,0:T(8,128)(2,1)}) custom-call(bf16[288,128]{1,0:T(8,128)(2,1)} %bitcast.8, s32[1,128]{1,0:T(1,128)} %seg.1, s32[1,128]{1,0:T(1,128)} %bitcast.15, f32[36,128]{1,0:T(8,128)} %bitcast.9, f32[36,128]{1,0:T(8,128)} %bitcast.10, bf16[4608,256]{1,0:T(8,128)(2,1)} %wq_hbm.1, ...), custom_call_target="tpu_custom_call" | custom-call | tf_op jit(solution)/shard_map/pallas_call | solution.py:672
  173.9 1.9 %copy.19 = bf16[288,1024]{1,0:T(8,128)(2,1)} copy(bf16[288,1024]{1,0:T(8,128)(2,1)} %get-tuple-element.12) | data formatting | bytes 1179648
  175.8 1.3 copy.20
  177.1 1.7 copy.21
